TPU v7x, 128 devices: a whole 4x4x4 slice. The times are simulated.
128 devices in a mesh: pts: 8 (over y, x_lo), py: 4 (over z), pz: 4 (over x_hi, core).
Axes of the slice: x: 4 (x_hi: 2, x_lo: 2; x = x_hi * 2 + x_lo), y: 4, z: 4, core: 2. Of those that a mesh axis runs over, the one named last changes fastest.
Arguments:
- xi_map: float32 [256, 256, 256], P('py', 'pz'), may hold values from -6 to 6
- basis: bfloat16 [3, 256, 256, 256], P(None, 'py', 'pz'), may hold values from -6 to 6
- point_index: int32 [16, 3], P('pts'), may hold values from 0 to 2, as said below
- conc_start: float32 [256, 256, 256], P(None, ('py', 'pz')), may hold values from 0.05 to 1
- well_mask: int32 [256, 256], replicated, may hold values 0 or 1
- profile: float32 [256], replicated, may hold values from 0.5 to 2
Outputs:
- expected_conc: float32 [256, 256, 256], P('pts', ('py', 'pz'))
Inputs may be any that keep to these rules, and one draw needn't show every extreme that they name: `point_index`: no two rows are equal; some row is all 0 and some row is all 2.
All inputs are finite; a program needn't handle non-finite values.
Results may differ from a plain program's by a relative error of at most 0.0003.
Values sent between devices are 32-bit elements; how exact they have to be, the bound alone decides.
A program may use at most 192 MiB of HBM per device.

v0:
```python
import functools

import jax
import jax.numpy as jnp
import ml_dtypes
import numpy as np
from jax import lax
from jax.experimental import pallas as pl
from jax.experimental.pallas import tpu as pltpu
from jax.sharding import PartitionSpec as P

MESH = pl.DeviceIdType.MESH
STEPS = 4
POINTS = 16
G = 256
NROUND = 10
ROOT3 = 1.7320508075688772
F32 = jnp.float32
BF16 = jnp.bfloat16
NT = (((1,), (1,)), ((), ()))


def split_table(table):
    table = np.asarray(table, np.float64)
    high = table.astype(np.float32).astype(ml_dtypes.bfloat16)
    low = (table - high.astype(np.float64)).astype(np.float32).astype(ml_dtypes.bfloat16)
    return high, low


def tables():
    spots = np.arange(G, dtype=np.float64)
    full = np.sqrt(2.0 / G) * np.cos(np.pi * (spots[:, None] + 0.5) * spots[None, :] / G)
    full[:, 0] *= np.sqrt(0.5)
    tz = np.zeros((G + 64, G))
    tz[4 : 4 + G] = full
    cy = np.zeros((8, 5, 8, G))
    for u in range(8):
        for t in range(5):
            for q in range(8):
                y = 32 * u - 8 + 5 * q + t
                if y >= 0:
                    cy[u, t, q] = full[y]
    cx = 0.5 * np.concatenate([full[0::2], full[1::2]], axis=0).T
    return split_table(tz), split_table(cy.reshape(320, G)), split_table(cx)


def halves(value):
    high = value.astype(BF16)
    low = (value - high.astype(F32)).astype(BF16)
    return high, low


def kernel(
    point,
    prof,
    xi_far,
    basis_far,
    tz,
    cy,
    cx,
    cz,
    mask,
    out,
    xi,
    basis,
    share,
    got1,
    rows2,
    got2,
    conc0,
    fields,
    carry,
    plane,
    wave,
    mine,
    listed,
    nodes,
    sums,
    parcel,
    landed,
    final,
    s1,
    r1,
    own1,
    s2,
    r2,
    own2,
    sc,
    rc,
    load,
    sn,
    rn,
    so,
    ro,
):
    pts = lax.axis_index("pts")
    i = lax.axis_index("py")
    pz = lax.axis_index("pz")
    yy, x_lo = pts // 2, pts % 2
    h, c = pz // 2, pz % 2
    xt = (x_lo + h) % 2
    u = 2 * i + c

    def at(i_, h_, c_):
        return {"pts": 2 * yy + (xt + h_) % 2, "py": i_, "pz": 2 * h_ + c_}

    barrier = pltpu.get_barrier_semaphore()
    peers = []
    for dp in range(8):
        for dh in range(2):
            for dc in range(2):
                if dp + dh + dc > 0:
                    peers.append({"pts": (pts + dp) % 8, "py": i, "pz": 2 * ((h + dh) % 2) + (c + dc) % 2})
    for di in range(1, 4):
        for dh in range(2):
            for dc in range(2):
                peers.append(at((i + di) % 4, (h + dh) % 2, (c + dc) % 2))
    for peer in peers:
        pl.semaphore_signal(barrier, inc=1, device_id=peer, device_id_type=MESH)

    def loads(q):
        copies = []
        for half in range(2):
            rows = pl.ds(pl.multiple_of(8 * q + 32 * half, 8), 8)
            copies.append(pltpu.make_async_copy(xi_far.at[rows], xi.at[rows], load.at[q, 2 * half]))
            copies.append(
                pltpu.make_async_copy(basis_far.at[:, rows], basis.at[:, rows], load.at[q, 2 * half + 1])
            )
        return copies

    def start_loads(q, _):
        for copy in loads(q):
            copy.start()
        return 0

    lax.fori_loop(0, 4, start_loads, 0)

    def slab_copy(to_h):
        return pltpu.make_async_remote_copy(
            src_ref=cz.at[:, pl.ds(16 * to_h, 20)],
            dst_ref=conc0.at[:, :, pl.ds(pl.multiple_of(8 + 16 * c, 8), 16)],
            send_sem=sc.at[to_h],
            recv_sem=rc.at[c],
            device_id=at(i, to_h, h),
            device_id_type=MESH,
        )

    def slab_local(to_h):
        return pltpu.make_async_copy(
            cz.at[:, pl.ds(16 * to_h, 20)],
            conc0.at[:, :, pl.ds(pl.multiple_of(8 + 16 * c, 8), 16)],
            rc.at[c],
        )

    above = 2 * i + h + 1

    def halo_copy(to_h):
        return pltpu.make_async_remote_copy(
            src_ref=cz.at[:, pl.ds(16 * to_h, 20), pl.ds(8, 8)],
            dst_ref=conc0.at[:, :, pl.ds(0, 8)],
            send_sem=sc.at[2 + to_h],
            recv_sem=rc.at[2],
            device_id=at((above // 2) % 4, to_h, above % 2),
            device_id_type=MESH,
        )

    def halo_local(to_h):
        return pltpu.make_async_copy(
            cz.at[:, pl.ds(16 * to_h, 20), pl.ds(8, 8)], conc0.at[:, :, pl.ds(0, 8)], rc.at[2]
        )

    def slab_here(to_h):
        return jnp.logical_and(h == to_h, c == to_h)

    def halo_some():
        return jnp.logical_and(c == 1, above < 8)

    for m in range(2):
        weight = 1.0
        for r in range(3):
            index = point[m, r]
            value = jnp.where(index == 0, -ROOT3, jnp.where(index == 1, 0.0, ROOT3))
            weight = weight * jnp.where(index == 1, 2.0 / 3.0, 1.0 / 6.0)
            mine[4 * m + r : 4 * m + r + 1, :] = jnp.full((1, 128), value, F32)
        mine[4 * m + 3 : 4 * m + 4, :] = jnp.full((1, 128), weight, F32)

    def node_copy(dp):
        return pltpu.make_async_remote_copy(
            src_ref=mine,
            dst_ref=listed.at[pts],
            send_sem=sn.at[dp],
            recv_sem=rn.at[dp],
            device_id={"pts": (pts + dp) % 8, "py": i, "pz": pz},
            device_id_type=MESH,
        )

    def greet():
        pl.semaphore_wait(barrier, len(peers))
        for dp in range(1, 8):
            node_copy(dp).start()
        listed[pts] = mine[...]
        for to_h in range(2):

            @pl.when(slab_here(to_h))
            def _():
                slab_local(to_h).start()

            @pl.when(jnp.logical_not(slab_here(to_h)))
            def _():
                slab_copy(to_h).start()

        @pl.when(jnp.logical_and(halo_some(), h == 0))
        def _():
            halo_local(0).start()

        @pl.when(jnp.logical_and(halo_some(), h == 1))
        def _():
            halo_copy(0).start()

        @pl.when(halo_some())
        def _():
            halo_copy(1).start()

        @pl.when(u == 0)
        def _():
            conc0[:, :, 0:8, :] = jnp.zeros((2, 20, 8, 128), F32)

    spot_b = (lax.broadcasted_iota(jnp.int32, (64, G), 0) + 64 * pz).astype(F32)
    spot_c = lax.broadcasted_iota(jnp.int32, (64, G), 1).astype(F32)
    wave[...] = 64.0 + spot_b * spot_b + spot_c * spot_c
    front = 64.0 * 0.9 * (32.0**1.5)

    def stage(step, _):
        amps = []
        for part in range(2):
            for half in range(2):
                a = (64 * i + 2 * step + part + 32 * half).astype(F32)
                amps.append(front / (wave[...] + a * a))
        for f in range(4):
            parts = []
            for part in range(2):
                for half in range(2):
                    row = 2 * step + part + 32 * half
                    value = xi[row] if f == 0 else basis[f - 1, row].astype(F32)
                    parts.append(value * amps[2 * part + half])
            high, low = halves(jnp.concatenate(parts, axis=0))
            both = jnp.dot(high, tz[...], preferred_element_type=F32)
            both += jnp.dot(low, tz[...], preferred_element_type=F32)
            both = both.T
            total = both[0:40] + both[48:88]
            for part in range(2):
                share[pl.ds(32 * f + 2 * step + part, 40, stride=128), :] = total[
                    :, 128 * part : 128 * part + 128
                ]
        return 0

    def stages(q, _):
        for copy in loads(q):
            copy.wait()
        return lax.fori_loop(4 * q, 4 * q + 4, stage, 0)

    lax.fori_loop(0, 1, stages, 0)
    greet()
    lax.fori_loop(1, 4, stages, 0)

    def first(k, d):
        to_h, to_c = (h + d // 2) % 2, (c + d % 2) % 2
        return pltpu.make_async_remote_copy(
            src_ref=share.at[pl.ds(pl.multiple_of((16 * to_h + 2 * k + to_c) * 128, 128), 128)],
            dst_ref=got1.at[k, pz],
            send_sem=s1.at[k, d],
            recv_sem=r1.at[k, d],
            device_id=at(i, to_h, to_c),
            device_id_type=MESH,
        )

    def first_own(k):
        return pltpu.make_async_copy(
            share.at[pl.ds(pl.multiple_of((16 * h + 2 * k + c) * 128, 128), 128)], got1.at[k, pz], own1.at[k]
        )

    def send_first(k, _):
        for d in (2, 3, 1):
            first(k, d).start()
        first_own(k).start()
        return 0

    lax.fori_loop(0, NROUND, send_first, 0)

    def second(k, d):
        to_i, to_c = (i + d // 2) % 4, (c + d % 2) % 2
        return pltpu.make_async_remote_copy(
            src_ref=rows2.at[k, 2 * to_i + to_c],
            dst_ref=got2.at[k, c, i],
            send_sem=s2.at[k, d],
            recv_sem=r2.at[k, d],
            device_id=at(to_i, h, to_c),
            device_id_type=MESH,
        )

    def second_own(k):
        return pltpu.make_async_copy(rows2.at[k, u], got2.at[k, c, i], own2.at[k])

    lane = lax.broadcasted_iota(jnp.int32, (128, 128), 1)
    lane_low = lane < 64
    lane8 = lax.broadcasted_iota(jnp.int32, (8, 128), 1)
    lane_some = lane8 > 0
    lane40 = lax.broadcasted_iota(jnp.int32, (40, 128), 1) < 64

    def b_contraction(k):
        for d in range(1, 4):
            first(k, d).wait_recv()
        first_own(k).wait()
        sides = [[], []]
        for pair in range(2):
            one, two = got1[k, 2 * pair], got1[k, 2 * pair + 1]
            sides[0].append(jnp.where(lane_low, one, pltpu.roll(two, 64, 1)))
            sides[1].append(jnp.where(lane_low, pltpu.roll(one, 64, 1), two))
        both = [jnp.concatenate(side, axis=1) for side in sides]
        rows = []
        for f in range(4):
            rows += [both[0][32 * f : 32 * f + 32], both[1][32 * f : 32 * f + 32]]
        high, low = halves(jnp.concatenate(rows, axis=0))
        for part in range(2):
            top = lax.dot_general(
                cy[160 * part : 160 * part + 160], high, NT, preferred_element_type=F32
            )
            top += lax.dot_general(
                cy[320 + 160 * part : 480 + 160 * part], high, NT, preferred_element_type=F32
            )
            top += lax.dot_general(
                cy[160 * part : 160 * part + 160], low, NT, preferred_element_type=F32
            )
            for slab in range(4):
                rows2[k, 4 * part + slab] = top[40 * slab : 40 * slab + 40]
        for d in (4, 5, 2, 6, 3, 7, 1):
            second(k, d).start()
        second_own(k).start()

    def a_contraction(k):
        for d in range(1, 8):
            second(k, d).wait_recv()
        second_own(k).wait()
        for core in range(2):
            rows = []
            for pair in range(2):
                cols = [[], []]
                for group in range(2):
                    one = got2[k, core, 2 * group, :, 128 * pair : 128 * pair + 128]
                    two = got2[k, core, 2 * group + 1, :, 128 * pair : 128 * pair + 128]
                    cols[0].append(jnp.where(lane40, one, pltpu.roll(two, 64, 1)))
                    cols[1].append(jnp.where(lane40, pltpu.roll(one, 64, 1), two))
                rows += [jnp.concatenate(col, axis=1) for col in cols]
            high, low = halves(jnp.concatenate(rows, axis=0))
            total = jnp.dot(high, cx[0:256], preferred_element_type=F32)
            total += jnp.dot(high, cx[256:512], preferred_element_type=F32)
            total += jnp.dot(low, cx[0:256], preferred_element_type=F32)
            fields[core] = total

    tiles = [(t, v) for t in range(5) for v in range(2)]

    def transport(k, core, halo):
        zz = 2 * k + core
        well = prof[zz]
        for t, v in tiles:
            plane[0, t, v] = conc0[v, zz, pl.ds(t, 8, stride=5), :]
            plane[1, t, v] = mask[v, 8 * t : 8 * t + 8, :] * well
            if not halo:
                plane[2, t, v] = jnp.zeros((8, 128), F32)
        steps = zz + 1 if halo else STEPS

        def one_point(n, _):
            node = [nodes[n, r] for r in range(3)]
            weight = nodes[n, 3]
            speed, keep, conc = {}, {}, {}
            for t, v in tiles:
                logs = [
                    fields[core, 40 * f + 8 * t : 40 * f + 8 * t + 8, 128 * v : 128 * v + 128]
                    for f in range(4)
                ]
                value = logs[0] + node[0] * logs[1] + node[1] * logs[2] + node[2] * logs[3]
                value = jnp.tanh(value)
                speed[t, v] = 0.125 + 0.125 * value
                keep[t, v] = 0.55 - 0.45 * value
                conc[t, v] = plane[0, t, v]
            for step in range(steps):
                last = halo and step == steps - 1
                flux = {tv: speed[tv] * conc[tv] for tv in tiles}
                for t, v in tiles:
                    if last:
                        carry[n, step, t, v] = flux[t, v]
                        continue
                    behind = carry[n, step, t, v]
                    carry[n, step, t, v] = flux[t, v]
                    prev_b = flux[t - 1, v] if t > 0 else pltpu.roll(flux[4, v], 1, 0)
                    prev_a = (
                        flux[t, 0]
                        if v == 1
                        else jnp.where(lane_some, pltpu.roll(flux[t, 1], 1, 1), 0.0)
                    )
                    conc[t, v] = (
                        keep[t, v] * conc[t, v]
                        + plane[1, t, v]
                        + behind
                        + prev_b
                        + 1.6 * prev_a
                    )
            if not halo:
                for t, v in tiles:
                    plane[2, t, v] += weight * conc[t, v]
            return 0

        lax.fori_loop(0, POINTS, one_point, 0)
        if not halo:
            for t, v in tiles:
                sums[v, pl.ds(16 * t + zz - 4, 8, stride=80), :] = plane[2, t, v]

    carry[...] = jnp.zeros(carry.shape, F32)
    lag = 2

    def wait_conc():
        for core in range(2):
            slab = pltpu.make_async_copy(
                cz.at[:, pl.ds(0, 20)], conc0.at[:, :, pl.ds(8 + 16 * core, 16)], rc.at[core]
            )
            slab.wait()

        @pl.when(u > 0)
        def _():
            pltpu.make_async_copy(
                cz.at[:, pl.ds(0, 20), pl.ds(8, 8)], conc0.at[:, :, pl.ds(0, 8)], rc.at[2]
            ).wait()

    def rounds(step, _):
        @pl.when(step < NROUND)
        def _():
            b_contraction(step)

        @pl.when(step >= lag)
        def _():
            a_contraction(step - lag)

        for early in range(2):

            @pl.when(step == lag + early)
            def _():
                for core in range(2):
                    transport(early, core, True)

        @pl.when(step >= lag + 2)
        def _():
            for core in range(2):
                transport(step - lag, core, False)

        return 0

    wait_conc()
    for dp in range(1, 8):
        node_copy(dp).wait_recv()
    for n in range(POINTS):
        for r in range(4):
            row = 4 * (n % 2) + r
            nodes[n, r] = jnp.broadcast_to(listed[n // 2, row : row + 1, :], (8, 128))
    lax.fori_loop(0, NROUND + lag, rounds, 0)

    granule = lax.broadcasted_iota(jnp.int32, (16, 128), 1) // 16

    def regroup(which, _):
        half, yg = which // 4, which % 4
        arrays = []
        for yy in range(4):
            for v in range(2):
                row = pl.multiple_of(16 * (8 + 16 * half + 4 * yg + yy), 16)
                arrays.append(sums[v, pl.ds(row, 16), :])
        for bit in (4, 2, 1):
            clear = (granule // bit) % 2 == 0
            for m in range(8):
                if m // bit % 2 == 0:
                    one, two = arrays[m], arrays[m + bit]
                    arrays[m] = jnp.where(clear, one, pltpu.roll(two, 16 * bit, 1))
                    arrays[m + bit] = jnp.where(clear, pltpu.roll(one, 128 - 16 * bit, 1), two)
        for p in range(8):
            parcel[p, half, yg] = arrays[p]
        return 0

    zr = pl.multiple_of(16 * (4 * yy + 2 * xt + h), 16)

    def home(dp, half):
        to = (pts + dp) % 8
        return pltpu.make_async_remote_copy(
            src_ref=parcel.at[to, half],
            dst_ref=landed.at[:, pl.ds(zr, 16)],
            send_sem=so.at[dp, half],
            recv_sem=ro.at[dp, h],
            device_id={"pts": to, "py": i, "pz": 2 * c + half},
            device_id_type=MESH,
        )

    def home_own(half):
        return pltpu.make_async_copy(parcel.at[pts, half], landed.at[:, pl.ds(zr, 16)], ro.at[0, h])

    for half in range(2):
        lax.fori_loop(4 * half, 4 * half + 4, regroup, 0)
        here = jnp.logical_and(c == h, c == half)

        @pl.when(here)
        def _():
            home_own(half).start()

        @pl.when(jnp.logical_not(here))
        def _():
            home(0, half).start()

        for dp in range(1, 8):
            home(dp, half).start()

    for dp in range(8):
        for from_h in range(2):
            pltpu.make_async_copy(
                parcel.at[0, 0], landed.at[:, pl.ds(0, 16)], ro.at[dp, from_h]
            ).wait()

    for yg in range(4):
        for zh in range(2):
            turned = landed[yg, 128 * zh : 128 * zh + 128, :].T
            for y in range(4):
                for v in range(2):
                    e = 16 * (2 * y + v)
                    final[zh, pl.ds(16 * v + 4 * yg + y, 16, stride=32), :] = turned[e : e + 16]
    for zh in range(2):
        out[:, 128 * zh : 128 * zh + 128] = final[zh]

    def drain(k, _):
        for d in range(1, 4):
            first(k, d).wait_send()
        for d in range(1, 8):
            second(k, d).wait_send()
        return 0

    lax.fori_loop(0, NROUND, drain, 0)
    for dp in range(1, 8):
        node_copy(dp).wait_send()
        for half in range(2):
            home(dp, half).wait_send()
    for half in range(2):

        @pl.when(jnp.logical_not(jnp.logical_and(c == h, c == half)))
        def _():
            home(0, half).wait_send()

    for to_h in range(2):

        @pl.when(jnp.logical_not(slab_here(to_h)))
        def _():
            slab_copy(to_h).wait_send()

    @pl.when(jnp.logical_and(halo_some(), h == 1))
    def _():
        halo_copy(0).wait_send()

    @pl.when(halo_some())
    def _():
        halo_copy(1).wait_send()


def local(xi_map, basis, point_index, conc_start, well_mask, profile):
    (tz_hi, tz_lo), (cy_hi, cy_lo), (cx_hi, cx_lo) = tables()
    pts = lax.axis_index("pts")
    i = lax.axis_index("py")
    pz = lax.axis_index("pz")
    yy, x_lo = pts // 2, pts % 2
    h, c = pz // 2, pz % 2
    xt = (x_lo + h) % 2
    g = 2 * yy + xt
    u = 2 * i + c

    tz = jnp.concatenate(
        [lax.dynamic_slice_in_dim(jnp.asarray(part), 32 * g, 48, 0) for part in (tz_hi, tz_lo)], axis=0
    )
    tz = jnp.pad(tz, ((0, 32), (0, 0))).T
    cy = jnp.concatenate([cy_hi, cy_lo], axis=0)
    cx = jnp.concatenate([cx_hi, cx_lo], axis=0)

    prof = 0.5 * lax.dynamic_slice_in_dim(jnp.pad(profile, (4, 0)), 16 * (2 * g + h), 20, 0)
    mask = lax.dynamic_slice_in_dim(jnp.pad(well_mask, ((0, 0), (8, 0))), 32 * u, 40, 1)
    mask = mask.astype(F32).reshape(128, 2, 8, 5).transpose(1, 3, 2, 0).reshape(2, 40, 128)
    cz = lax.dynamic_slice_in_dim(jnp.pad(conc_start, ((0, 0), (0, 0), (4, 0))), 32 * g, 36, 2)
    cz = cz.reshape(128, 2, 16, 36).transpose(1, 3, 2, 0)

    vmem = pl.BlockSpec(memory_space=pltpu.VMEM)
    smem = pl.BlockSpec(memory_space=pltpu.SMEM)
    dma = pltpu.SemaphoreType.DMA
    far = pl.BlockSpec(memory_space=pl.ANY)
    total = pl.pallas_call(
        kernel,
        out_shape=jax.ShapeDtypeStruct((512, 256), F32),
        in_specs=[smem, smem, far, far] + [vmem] * 5,
        out_specs=vmem,
        scratch_shapes=[
            pltpu.VMEM((64, 64, 256), F32),
            pltpu.VMEM((3, 64, 64, 256), BF16),
            pltpu.VMEM((40 * 128, 128), F32),
            pltpu.VMEM((NROUND, 4, 128, 128), F32),
            pltpu.VMEM((NROUND, 8, 40, 256), F32),
            pltpu.VMEM((NROUND, 2, 4, 40, 256), F32),
            pltpu.VMEM((2, 20, 40, 128), F32),
            pltpu.VMEM((2, 160, 256), F32),
            pltpu.VMEM((POINTS, STEPS, 5, 2, 8, 128), F32),
            pltpu.VMEM((3, 5, 2, 8, 128), F32),
            pltpu.VMEM((64, 256), F32),
            pltpu.VMEM((8, 128), F32),
            pltpu.VMEM((8, 8, 128), F32),
            pltpu.VMEM((POINTS, 4, 8, 128), F32),
            pltpu.VMEM((2, 640, 128), F32),
            pltpu.VMEM((8, 2, 4, 16, 128), F32),
            pltpu.VMEM((4, 256, 128), F32),
            pltpu.VMEM((2, 512, 128), F32),
            dma((NROUND, 4)),
            dma((NROUND, 4)),
            dma((NROUND,)),
            dma((NROUND, 8)),
            dma((NROUND, 8)),
            dma((NROUND,)),
            dma((4,)),
            dma((3,)),
            dma((4, 4)),
            dma((8,)),
            dma((8,)),
            dma((8, 2)),
            dma((8, 2)),
        ],
        compiler_params=pltpu.CompilerParams(
            collective_id=0, has_side_effects=True, vmem_limit_bytes=60 * 2**20
        ),
    )(point_index, prof, xi_map, basis, tz, cy, cx, cz, mask)
    return total.reshape(32, 16, 256)


def solution(mesh):
    placed = (
        P("py", "pz", None),
        P(None, "py", "pz", None),
        P("pts", None),
        P(None, ("py", "pz"), None),
        P(),
        P(),
    )
    return jax.shard_map(
        local, mesh=mesh, in_specs=placed, out_specs=P("pts", ("py", "pz"), None), check_vma=False
    )
```

profile of v0, /device:TPU:1, one launch (start us, length us, event | category | flops | bytes accessed | tf_op | source)
XLA Modules:
  0.0 117.7 jit_solution(11040655161709918084)
XLA Ops:
  0.0 0.0 copy-start
  0.0 2.9 %pad_dynamic-slice_fusion = f32[256,16,36]{2,1,0:T(8,128)S(1)} fusion(s32[]{:T(128)S(6)} %select_n.41, f32[256,16,256]{2,1,0:T(8,128)} %param.15), kind=kLoop, calls=%fused_computation | loop fusion | bytes 4784132 | tf_op jit(solution)/shard_map/dynamic_slice | solution.py:587
  2.9 0.0 copy-start.1
  2.9 2.3 %copy.14 = f32[128,2,16,36]{0,2,3,1:T(8,128)} copy(f32[128,2,16,36]{3,2,1,0:T(8,128)S(1)} %bitcast.7) | data formatting | bytes 1179648 | tf_op jit(solution)/shard_map/reshape | solution.py:588
  5.2 0.0 copy-done
  5.2 0.1 fusion
  5.3 0.3 reshape.13
  5.6 1.1 copy.15
  6.7 1.1 constant_dynamic-slice_fusion
  7.8 0.7 fusion.4.tz
  8.5 0.0 copy-done.1
  8.5 0.6 fusion.5.prof
  9.1 106.7 %shard_map.118 = f32[512,256]{1,0:T(8,128)} custom-call(s32[2,3]{1,0:T(2,128)} %point.1, f32[20]{0:T(128)} %fusion.5.prof, f32[64,64,256]{2,1,0:T(8,128)} %xi_far.1, bf16[3,64,64,256]{3,2,1,0:T(8,128)(2,1)} %basis_far.1, bf16[256,128]{1,0:T(8,128)(2,1)} %fusion.4.tz, bf16[640,256]{1,0:T(8,128)(2,1)} %constant.96.cy, bf16[512,256]{1,0:T(8,128)(2,1)} %constant.97.cx, ...), custom_call_target="tpu_custom_call" | custom-call | tf_op jit(solution)/shard_map/pallas_call | solution.py:594
  115.8 1.9 %copy.17 = f32[32,16,256]{2,1,0:T(8,128)} copy(f32[32,16,256]{2,1,0:T(8,128)} %bitcast.10) | data formatting | bytes 1048576
Async XLA Ops:
  0.0 5.2 %copy-start = (s32[256,256]{1,0:T(8,128)S(1)}, s32[256,256]{1,0:T(8,128)}, u32[]{:S(2)}) copy-start(s32[256,256]{1,0:T(8,128)} %param.16) | copy-start | bytes 786436
  2.9 5.6 %copy-start.1 = (f32[256]{0:T(256)S(1)}, f32[256]{0:T(256)}, u32[]{:S(2)}) copy-start(f32[256]{0:T(256)} %param.17) | copy-start | bytes 3076
where the time goes:
time: 118 us
  Pallas kernels  107 us (91%)
  local copies, waits for them, and re-layouts  9.48 us (8%)
  other arithmetic  1.44 us (1%)
    pallas_call x1, Pallas kernels, local(): pl.pallas_call(kernel, out_shape=jax.ShapeDtypeStruct((512, 256), F32), i...  107 us
    dynamic_slice x1, local copies, waits for them, and re-layouts, local(): lax.dynamic_slice_in_dim(jnp.pad(conc_start, ((0, 0), (0, 0), (4, 0))), 3...  2.88 us

commit v1 on v0

--- a/solution.py
+++ b/solution.py
@@ -12,6 +12,7 @@
 MESH = pl.DeviceIdType.MESH
 STEPS = 4
 POINTS = 16
+BATCH = 2
 G = 256
 NROUND = 10
 ROOT3 = 1.7320508075688772
@@ -321,18 +322,11 @@
         for f in range(4):
             rows += [both[0][32 * f : 32 * f + 32], both[1][32 * f : 32 * f + 32]]
         high, low = halves(jnp.concatenate(rows, axis=0))
-        for part in range(2):
-            top = lax.dot_general(
-                cy[160 * part : 160 * part + 160], high, NT, preferred_element_type=F32
-            )
-            top += lax.dot_general(
-                cy[320 + 160 * part : 480 + 160 * part], high, NT, preferred_element_type=F32
-            )
-            top += lax.dot_general(
-                cy[160 * part : 160 * part + 160], low, NT, preferred_element_type=F32
-            )
-            for slab in range(4):
-                rows2[k, 4 * part + slab] = top[40 * slab : 40 * slab + 40]
+        both = lax.dot_general(cy[...], high, NT, preferred_element_type=F32)
+        rest = lax.dot_general(cy[0:320], low, NT, preferred_element_type=F32)
+        total = both[0:320] + both[320:640] + rest
+        for slab in range(8):
+            rows2[k, slab] = total[40 * slab : 40 * slab + 40]
         for d in (4, 5, 2, 6, 3, 7, 1):
             second(k, d).start()
         second_own(k).start()
@@ -341,8 +335,8 @@
         for d in range(1, 8):
             second(k, d).wait_recv()
         second_own(k).wait()
+        rows = []
         for core in range(2):
-            rows = []
             for pair in range(2):
                 cols = [[], []]
                 for group in range(2):
@@ -351,11 +345,14 @@
                     cols[0].append(jnp.where(lane40, one, pltpu.roll(two, 64, 1)))
                     cols[1].append(jnp.where(lane40, pltpu.roll(one, 64, 1), two))
                 rows += [jnp.concatenate(col, axis=1) for col in cols]
-            high, low = halves(jnp.concatenate(rows, axis=0))
-            total = jnp.dot(high, cx[0:256], preferred_element_type=F32)
-            total += jnp.dot(high, cx[256:512], preferred_element_type=F32)
-            total += jnp.dot(low, cx[0:256], preferred_element_type=F32)
-            fields[core] = total
+        high, low = halves(jnp.concatenate(rows, axis=0))
+        total = jnp.dot(high, cx[0:256], preferred_element_type=F32)
+        total += jnp.dot(low, cx[0:256], preferred_element_type=F32)
+        total += jnp.dot(high, cx[256:512], preferred_element_type=F32)
+        for core in range(2):
+            for f in range(4):
+                row = 160 * core + 40 * f
+                fields[core, f] = total[row : row + 40]
 
     tiles = [(t, v) for t in range(5) for v in range(2)]
 
@@ -369,48 +366,51 @@
                 plane[2, t, v] = jnp.zeros((8, 128), F32)
         steps = zz + 1 if halo else STEPS
 
-        def one_point(n, _):
-            node = [nodes[n, r] for r in range(3)]
-            weight = nodes[n, 3]
-            speed, keep, conc = {}, {}, {}
-            for t, v in tiles:
-                logs = [
-                    fields[core, 40 * f + 8 * t : 40 * f + 8 * t + 8, 128 * v : 128 * v + 128]
-                    for f in range(4)
-                ]
-                value = logs[0] + node[0] * logs[1] + node[1] * logs[2] + node[2] * logs[3]
-                value = jnp.tanh(value)
-                speed[t, v] = 0.125 + 0.125 * value
-                keep[t, v] = 0.55 - 0.45 * value
-                conc[t, v] = plane[0, t, v]
+        def some_points(group, _):
+            each = range(BATCH)
+            speed, conc = [{} for _ in each], [{} for _ in each]
+            for m in each:
+                n = BATCH * group + m
+                node = [nodes[n, r] for r in range(3)]
+                for t, v in tiles:
+                    logs = [
+                        fields[core, f, 8 * t : 8 * t + 8, 128 * v : 128 * v + 128] for f in range(4)
+                    ]
+                    value = logs[0] + node[0] * logs[1] + node[1] * logs[2] + node[2] * logs[3]
+                    speed[m][t, v] = 0.125 + 0.125 * jnp.tanh(value)
+                    conc[m][t, v] = plane[0, t, v]
             for step in range(steps):
                 last = halo and step == steps - 1
-                flux = {tv: speed[tv] * conc[tv] for tv in tiles}
+                flux = [{tv: speed[m][tv] * conc[m][tv] for tv in tiles} for m in each]
                 for t, v in tiles:
-                    if last:
-                        carry[n, step, t, v] = flux[t, v]
-                        continue
-                    behind = carry[n, step, t, v]
-                    carry[n, step, t, v] = flux[t, v]
-                    prev_b = flux[t - 1, v] if t > 0 else pltpu.roll(flux[4, v], 1, 0)
-                    prev_a = (
-                        flux[t, 0]
-                        if v == 1
-                        else jnp.where(lane_some, pltpu.roll(flux[t, 1], 1, 1), 0.0)
-                    )
-                    conc[t, v] = (
-                        keep[t, v] * conc[t, v]
-                        + plane[1, t, v]
-                        + behind
-                        + prev_b
-                        + 1.6 * prev_a
-                    )
+                    for m in each:
+                        n = BATCH * group + m
+                        here = flux[m][t, v]
+                        if last:
+                            carry[n, step, t, v] = here
+                            continue
+                        behind = carry[n, step, t, v]
+                        carry[n, step, t, v] = here
+                        prev_b = flux[m][t - 1, v] if t > 0 else pltpu.roll(flux[m][4, v], 1, 0)
+                        prev_a = (
+                            flux[m][t, 0]
+                            if v == 1
+                            else jnp.where(lane_some, pltpu.roll(flux[m][t, 1], 1, 1), 0.0)
+                        )
+                        conc[m][t, v] = (
+                            (conc[m][t, v] - 3.6 * here)
+                            + (plane[1, t, v] + behind)
+                            + (prev_b + 1.6 * prev_a)
+                        )
             if not halo:
                 for t, v in tiles:
-                    plane[2, t, v] += weight * conc[t, v]
+                    part = nodes[BATCH * group, 3] * conc[0][t, v]
+                    for m in range(1, BATCH):
+                        part += nodes[BATCH * group + m, 3] * conc[m][t, v]
+                    plane[2, t, v] += part
             return 0
 
-        lax.fori_loop(0, POINTS, one_point, 0)
+        lax.fori_loop(0, POINTS // BATCH, some_points, 0)
         if not halo:
             for t, v in tiles:
                 sums[v, pl.ds(16 * t + zz - 4, 8, stride=80), :] = plane[2, t, v]
@@ -604,7 +604,7 @@
             pltpu.VMEM((NROUND, 8, 40, 256), F32),
             pltpu.VMEM((NROUND, 2, 4, 40, 256), F32),
             pltpu.VMEM((2, 20, 40, 128), F32),
-            pltpu.VMEM((2, 160, 256), F32),
+            pltpu.VMEM((2, 4, 40, 256), F32),
             pltpu.VMEM((POINTS, STEPS, 5, 2, 8, 128), F32),
             pltpu.VMEM((3, 5, 2, 8, 128), F32),
             pltpu.VMEM((64, 256), F32),

time: 118 us -> 95.9 us (0.81)
  Pallas kernels: 107 us -> 84.7 us
    pallas_call x1, Pallas kernels: 107 us -> 84.7 us  [local(): pl.pallas_call(kernel, out_shape=jax.ShapeDtypeStruct((512, 256), F32), i...]
where the time goes in v1:
time: 95.9 us; the launch traced here: 95.7 us
  Pallas kernels  84.7 us (88%)
  local copies, waits for them, and re-layouts  9.48 us (10%)
  other arithmetic  1.44 us (2%)
    pallas_call x1, Pallas kernels, local(): pl.pallas_call(kernel, out_shape=jax.ShapeDtypeStruct((512, 256), F32), i...  84.7 us
    dynamic_slice x1, local copies, waits for them, and re-layouts, local(): lax.dynamic_slice_in_dim(jnp.pad(conc_start, ((0, 0), (0, 0), (4, 0))), 3...  2.88 us
    reshape x1, local copies, waits for them, and re-layouts, local(): cz = cz.reshape(128, 2, 16, 36).transpose(1, 3, 2, 0)  2.28 us

profile of v1, /device:TPU:1, one launch (start us, length us, event | category | flops | bytes accessed | tf_op | source)
XLA Modules:
  0.0 95.7 jit_solution(5831939623383978570)
XLA Ops:
  0.0 0.0 copy-start
  0.0 2.9 %pad_dynamic-slice_fusion = f32[256,16,36]{2,1,0:T(8,128)S(1)} fusion(s32[]{:T(128)S(6)} %select_n.41, f32[256,16,256]{2,1,0:T(8,128)} %param.15), kind=kLoop, calls=%fused_computation | loop fusion | bytes 4784132 | tf_op jit(solution)/shard_map/dynamic_slice | solution.py:587
  2.9 0.0 copy-start.1
  2.9 2.3 %copy.14 = f32[128,2,16,36]{0,2,3,1:T(8,128)} copy(f32[128,2,16,36]{3,2,1,0:T(8,128)S(1)} %bitcast.7) | data formatting | bytes 1179648 | tf_op jit(solution)/shard_map/reshape | solution.py:588
  5.2 0.0 copy-done
  5.2 0.1 fusion
  5.3 0.3 reshape.13
  5.6 1.1 %copy.15 = f32[2,5,8,128]{3,2,1,0:T(8,128)} copy(f32[2,5,8,128]{1,2,0,3:T(8,128)S(1)} %bitcast.8) | data formatting | bytes 81920 | tf_op jit(solution)/shard_map/transpose | solution.py:586
  6.7 1.1 %constant_dynamic-slice_fusion = (bf16[48,256]{0,1:T(8,128)(2,1)S(1)}, bf16[48,256]{0,1:T(8,128)(2,1)S(1)}) fusion(bf16[320,256]{0,1:T(8,128)(2,1)} %constant.82.clone, s32[]{:T(128)S(6)} %select_n.40, bf16[320,256]{0,1:T(8,128)(2,1)} %constant.81.clone), kind=kLoop, calls=%fused_computation.9 | loop fusion | bytes 98308 | tf_op jit(solution)/shard_map/dynamic_slice | solution.py:578
  7.8 0.7 fusion.4.tz
  8.5 0.0 copy-done.1
  8.5 0.6 fusion.5.prof
  9.1 84.7 %shard_map.118 = f32[512,256]{1,0:T(8,128)} custom-call(s32[2,3]{1,0:T(2,128)} %point.1, f32[20]{0:T(128)} %fusion.5.prof, f32[64,64,256]{2,1,0:T(8,128)} %xi_far.1, bf16[3,64,64,256]{3,2,1,0:T(8,128)(2,1)} %basis_far.1, bf16[256,128]{1,0:T(8,128)(2,1)} %fusion.4.tz, bf16[640,256]{1,0:T(8,128)(2,1)} %constant.96.cy, bf16[512,256]{1,0:T(8,128)(2,1)} %constant.97.cx, ...), custom_call_target="tpu_custom_call" | custom-call | tf_op jit(solution)/shard_map/pallas_call | solution.py:594
  93.8 1.9 %copy.17 = f32[32,16,256]{2,1,0:T(8,128)} copy(f32[32,16,256]{2,1,0:T(8,128)} %bitcast.10) | data formatting | bytes 1048576
Async XLA Ops:
  0.0 5.2 %copy-start = (s32[256,256]{1,0:T(8,128)S(1)}, s32[256,256]{1,0:T(8,128)}, u32[]{:S(2)}) copy-start(s32[256,256]{1,0:T(8,128)} %param.16) | copy-start | bytes 786436
  2.9 5.6 %copy-start.1 = (f32[256]{0:T(256)S(1)}, f32[256]{0:T(256)}, u32[]{:S(2)}) copy-start(f32[256]{0:T(256)} %param.17) | copy-start | bytes 3076

commit v2 on v1

--- a/solution.py
+++ b/solution.py
@@ -12,7 +12,7 @@
 MESH = pl.DeviceIdType.MESH
 STEPS = 4
 POINTS = 16
-BATCH = 2
+BATCH = 4
 G = 256
 NROUND = 10
 ROOT3 = 1.7320508075688772

time: 95.9 us -> 89.7 us (0.935)
  Pallas kernels: 84.7 us -> 78.5 us
    pallas_call x1, Pallas kernels: 84.7 us -> 78.5 us  [local(): pl.pallas_call(kernel, out_shape=jax.ShapeDtypeStruct((512, 256), F32), i...]
where the time goes in v2:
time: 89.7 us; the launch traced here: 89.5 us
  Pallas kernels  78.5 us (88%)
  local copies, waits for them, and re-layouts  9.48 us (11%)
  other arithmetic  1.44 us (2%)
    pallas_call x1, Pallas kernels, local(): pl.pallas_call(kernel, out_shape=jax.ShapeDtypeStruct((512, 256), F32), i...  78.5 us
    dynamic_slice x1, local copies, waits for them, and re-layouts, local(): lax.dynamic_slice_in_dim(jnp.pad(conc_start, ((0, 0), (0, 0), (4, 0))), 3...  2.88 us
    reshape x1, local copies, waits for them, and re-layouts, local(): cz = cz.reshape(128, 2, 16, 36).transpose(1, 3, 2, 0)  2.28 us
    unnamed x5, local copies, waits for them, and re-layouts  1.88 us

profile of v2, /device:TPU:1, one launch (start us, length us, event | category | flops | bytes accessed | tf_op | source)
XLA Modules:
  0.0 89.5 jit_solution(13089118255297627659)
XLA Ops:
  0.0 0.0 copy-start
  0.0 2.9 %pad_dynamic-slice_fusion = f32[256,16,36]{2,1,0:T(8,128)S(1)} fusion(s32[]{:T(128)S(6)} %select_n.41, f32[256,16,256]{2,1,0:T(8,128)} %param.15), kind=kLoop, calls=%fused_computation | loop fusion | bytes 4784132 | tf_op jit(solution)/shard_map/dynamic_slice | solution.py:587
  2.9 0.0 copy-start.1
  2.9 2.3 %copy.14 = f32[128,2,16,36]{0,2,3,1:T(8,128)} copy(f32[128,2,16,36]{3,2,1,0:T(8,128)S(1)} %bitcast.7) | data formatting | bytes 1179648 | tf_op jit(solution)/shard_map/reshape | solution.py:588
  5.2 0.0 copy-done
  5.2 0.1 fusion
  5.3 0.3 reshape.13
  5.6 1.1 %copy.15 = f32[2,5,8,128]{3,2,1,0:T(8,128)} copy(f32[2,5,8,128]{1,2,0,3:T(8,128)S(1)} %bitcast.8) | data formatting | bytes 81920 | tf_op jit(solution)/shard_map/transpose | solution.py:586
  6.7 1.1 %constant_dynamic-slice_fusion = (bf16[48,256]{0,1:T(8,128)(2,1)S(1)}, bf16[48,256]{0,1:T(8,128)(2,1)S(1)}) fusion(bf16[320,256]{0,1:T(8,128)(2,1)} %constant.82.clone, s32[]{:T(128)S(6)} %select_n.40, bf16[320,256]{0,1:T(8,128)(2,1)} %constant.81.clone), kind=kLoop, calls=%fused_computation.9 | loop fusion | bytes 98308 | tf_op jit(solution)/shard_map/dynamic_slice | solution.py:578
  7.8 0.7 fusion.4.tz
  8.5 0.0 copy-done.1
  8.5 0.6 fusion.5.prof
  9.1 78.5 %shard_map.118 = f32[512,256]{1,0:T(8,128)} custom-call(s32[2,3]{1,0:T(2,128)} %point.1, f32[20]{0:T(128)} %fusion.5.prof, f32[64,64,256]{2,1,0:T(8,128)} %xi_far.1, bf16[3,64,64,256]{3,2,1,0:T(8,128)(2,1)} %basis_far.1, bf16[256,128]{1,0:T(8,128)(2,1)} %fusion.4.tz, bf16[640,256]{1,0:T(8,128)(2,1)} %constant.96.cy, bf16[512,256]{1,0:T(8,128)(2,1)} %constant.97.cx, ...), custom_call_target="tpu_custom_call" | custom-call | tf_op jit(solution)/shard_map/pallas_call | solution.py:594
  87.6 1.9 %copy.17 = f32[32,16,256]{2,1,0:T(8,128)} copy(f32[32,16,256]{2,1,0:T(8,128)} %bitcast.10) | data formatting | bytes 1048576
Async XLA Ops:
  0.0 5.2 %copy-start = (s32[256,256]{1,0:T(8,128)S(1)}, s32[256,256]{1,0:T(8,128)}, u32[]{:S(2)}) copy-start(s32[256,256]{1,0:T(8,128)} %param.16) | copy-start | bytes 786436
  2.9 5.6 %copy-start.1 = (f32[256]{0:T(256)S(1)}, f32[256]{0:T(256)}, u32[]{:S(2)}) copy-start(f32[256]{0:T(256)} %param.17) | copy-start | bytes 3076

commit v3 on v2

--- a/solution.py
+++ b/solution.py
@@ -15,6 +15,7 @@
 BATCH = 4
 G = 256
 NROUND = 10
+EARLY = 4
 ROOT3 = 1.7320508075688772
 F32 = jnp.float32
 BF16 = jnp.bfloat16
@@ -32,8 +33,14 @@
     spots = np.arange(G, dtype=np.float64)
     full = np.sqrt(2.0 / G) * np.cos(np.pi * (spots[:, None] + 0.5) * spots[None, :] / G)
     full[:, 0] *= np.sqrt(0.5)
-    tz = np.zeros((G + 64, G))
-    tz[4 : 4 + G] = full
+    tz = np.zeros((8, 40, G))
+    for g in range(8):
+        for par in range(2):
+            for w in range(18):
+                z = 32 * g - 4 + 2 * w + par
+                if z >= 0:
+                    tz[g, 20 * par + w] = full[z]
+    tz = tz.transpose(0, 2, 1)
     cy = np.zeros((8, 5, 8, G))
     for u in range(8):
         for t in range(5):
@@ -56,11 +63,11 @@
     prof,
     xi_far,
     basis_far,
-    tz,
+    conc_far,
+    mask_far,
+    tz_far,
     cy,
     cx,
-    cz,
-    mask,
     out,
     xi,
     basis,
@@ -80,6 +87,16 @@
     parcel,
     landed,
     final,
+    tz,
+    start,
+    turned_z,
+    cz_flat,
+    wells,
+    turned_y,
+    mask,
+    s0,
+    r0,
+    own0,
     s1,
     r1,
     own1,
@@ -89,6 +106,7 @@
     sc,
     rc,
     load,
+    prep,
     sn,
     rn,
     so,
@@ -101,6 +119,8 @@
     h, c = pz // 2, pz % 2
     xt = (x_lo + h) % 2
     u = 2 * i + c
+    g = 2 * yy + xt
+    cz = cz_flat.reshape(2, 40, 16, 128)
 
     def at(i_, h_, c_):
         return {"pts": 2 * yy + (xt + h_) % 2, "py": i_, "pz": 2 * h_ + c_}
@@ -134,7 +154,28 @@
             copy.start()
         return 0
 
+    def load_conc(zh):
+        return pltpu.make_async_copy(
+            conc_far.at[:, pl.ds(128 * zh, 128)], start.at[zh], prep.at[zh]
+        )
+
+    def load_mask(yh):
+        return pltpu.make_async_copy(
+            mask_far.at[:, pl.ds(128 * yh, 128)], wells.at[yh], prep.at[2 + yh]
+        )
+
+    load_tz = pltpu.make_async_copy(tz_far.at[g], tz, prep.at[4])
+    some_z = [g <= 4, g >= 4]
+    for zh in range(2):
+
+        @pl.when(some_z[zh])
+        def _():
+            load_conc(zh).start()
+
+    load_tz.start()
     lax.fori_loop(0, 4, start_loads, 0)
+    for yh in range(2):
+        load_mask(yh).start()
 
     def slab_copy(to_h):
         return pltpu.make_async_remote_copy(
@@ -194,6 +235,40 @@
             device_id={"pts": (pts + dp) % 8, "py": i, "pz": pz},
             device_id_type=MESH,
         )
+
+    turned_z[:, 0:8, :] = jnp.zeros((2, 8, 128), F32)
+    for zh in range(2):
+
+        @pl.when(some_z[zh])
+        def _():
+            load_conc(zh).wait()
+
+    def turn_conc(y, _):
+        for zh in range(2):
+
+            @pl.when(some_z[zh])
+            def _():
+                for v in range(2):
+                    turned_z[v, 4 + 128 * zh : 132 + 128 * zh, :] = start[
+                        zh, pl.ds(16 * v + y, 128, stride=32), :
+                    ].T
+
+        for v in range(2):
+            cz_flat[v, pl.ds(y, 40, stride=16), :] = turned_z[v, pl.ds(pl.multiple_of(32 * g, 32), 40), :]
+        return 0
+
+    lax.fori_loop(0, 16, turn_conc, 0)
+
+    def turn_mask():
+        turned_y[:, 0:8, :] = jnp.zeros((2, 8, 128), F32)
+        for yh in range(2):
+            load_mask(yh).wait()
+            for v in range(2):
+                block = wells[yh, pl.ds(v, 128, stride=2), :].astype(F32)
+                turned_y[v, 8 + 128 * yh : 136 + 128 * yh, :] = 0.5 * block.T
+        for v in range(2):
+            for t in range(5):
+                mask[v, 8 * t : 8 * t + 8, :] = turned_y[v, pl.ds(32 * u + t, 8, stride=5), :]
 
     def greet():
         pl.semaphore_wait(barrier, len(peers))
@@ -248,7 +323,7 @@
             both = jnp.dot(high, tz[...], preferred_element_type=F32)
             both += jnp.dot(low, tz[...], preferred_element_type=F32)
             both = both.T
-            total = both[0:40] + both[48:88]
+            total = both[0:40] + both[40:80]
             for part in range(2):
                 share[pl.ds(32 * f + 2 * step + part, 40, stride=128), :] = total[
                     :, 128 * part : 128 * part + 128
@@ -258,16 +333,42 @@
     def stages(q, _):
         for copy in loads(q):
             copy.wait()
-        return lax.fori_loop(4 * q, 4 * q + 4, stage, 0)
-
-    lax.fori_loop(0, 1, stages, 0)
+        lax.fori_loop(4 * q, 4 * q + 4, stage, 0)
+        for d in (2, 3, 1):
+            early(q, d).start()
+        early_own(q).start()
+        return 0
+
+    blocks = share.reshape(40, 4, 32, 128)
+
+    def early_parts(q, to_h, to_c):
+        rows = pl.ds(pl.multiple_of(8 * q, 8), 8)
+        src = blocks.at[pl.ds(20 * to_c + 8 * to_h, EARLY), :, rows]
+        return src, got1.at[pl.ds(0, EARLY), pz, :, rows]
+
+    def early(q, d):
+        to_h, to_c = (h + d // 2) % 2, (c + d % 2) % 2
+        src, dst = early_parts(q, to_h, to_c)
+        return pltpu.make_async_remote_copy(
+            src_ref=src,
+            dst_ref=dst,
+            send_sem=s0.at[q, d],
+            recv_sem=r0.at[q, d],
+            device_id=at(i, to_h, to_c),
+            device_id_type=MESH,
+        )
+
+    def early_own(q):
+        return pltpu.make_async_copy(*early_parts(q, h, c), own0.at[q])
+
     greet()
-    lax.fori_loop(1, 4, stages, 0)
+    load_tz.wait()
+    lax.fori_loop(0, 4, stages, 0)
 
     def first(k, d):
         to_h, to_c = (h + d // 2) % 2, (c + d % 2) % 2
         return pltpu.make_async_remote_copy(
-            src_ref=share.at[pl.ds(pl.multiple_of((16 * to_h + 2 * k + to_c) * 128, 128), 128)],
+            src_ref=blocks.at[20 * to_c + 8 * to_h + k],
             dst_ref=got1.at[k, pz],
             send_sem=s1.at[k, d],
             recv_sem=r1.at[k, d],
@@ -276,9 +377,7 @@
         )
 
     def first_own(k):
-        return pltpu.make_async_copy(
-            share.at[pl.ds(pl.multiple_of((16 * h + 2 * k + c) * 128, 128), 128)], got1.at[k, pz], own1.at[k]
-        )
+        return pltpu.make_async_copy(blocks.at[20 * c + 8 * h + k], got1.at[k, pz], own1.at[k])
 
     def send_first(k, _):
         for d in (2, 3, 1):
@@ -286,7 +385,7 @@
         first_own(k).start()
         return 0
 
-    lax.fori_loop(0, NROUND, send_first, 0)
+    lax.fori_loop(EARLY, NROUND, send_first, 0)
 
     def second(k, d):
         to_i, to_c = (i + d // 2) % 4, (c + d % 2) % 2
@@ -309,12 +408,22 @@
     lane40 = lax.broadcasted_iota(jnp.int32, (40, 128), 1) < 64
 
     def b_contraction(k):
-        for d in range(1, 4):
-            first(k, d).wait_recv()
-        first_own(k).wait()
+        @pl.when(k == 0)
+        def _():
+            for q in range(4):
+                for d in range(1, 4):
+                    early(q, d).wait_recv()
+                early_own(q).wait()
+
+        @pl.when(k >= EARLY)
+        def _():
+            for d in range(1, 4):
+                first(k, d).wait_recv()
+            first_own(k).wait()
+
         sides = [[], []]
         for pair in range(2):
-            one, two = got1[k, 2 * pair], got1[k, 2 * pair + 1]
+            one, two = (got1[k, 2 * pair + m].reshape(128, 128) for m in range(2))
             sides[0].append(jnp.where(lane_low, one, pltpu.roll(two, 64, 1)))
             sides[1].append(jnp.where(lane_low, pltpu.roll(one, 64, 1), two))
         both = [jnp.concatenate(side, axis=1) for side in sides]
@@ -358,7 +467,8 @@
 
     def transport(k, core, halo):
         zz = 2 * k + core
-        well = prof[zz]
+        spot_z = 16 * (2 * g + h) - 4 + zz
+        well = jnp.where(spot_z >= 0, prof[jnp.maximum(spot_z, 0)], 0.0)
         for t, v in tiles:
             plane[0, t, v] = conc0[v, zz, pl.ds(t, 8, stride=5), :]
             plane[1, t, v] = mask[v, 8 * t : 8 * t + 8, :] * well
@@ -454,6 +564,7 @@
 
         return 0
 
+    turn_mask()
     wait_conc()
     for dp in range(1, 8):
         node_copy(dp).wait_recv()
@@ -531,8 +642,16 @@
         out[:, 128 * zh : 128 * zh + 128] = final[zh]
 
     def drain(k, _):
-        for d in range(1, 4):
-            first(k, d).wait_send()
+        @pl.when(k >= EARLY)
+        def _():
+            for d in range(1, 4):
+                first(k, d).wait_send()
+
+        @pl.when(k < 4)
+        def _():
+            for d in range(1, 4):
+                early(k, d).wait_send()
+
         for d in range(1, 8):
             second(k, d).wait_send()
         return 0
@@ -565,27 +684,9 @@
 
 def local(xi_map, basis, point_index, conc_start, well_mask, profile):
     (tz_hi, tz_lo), (cy_hi, cy_lo), (cx_hi, cx_lo) = tables()
-    pts = lax.axis_index("pts")
-    i = lax.axis_index("py")
-    pz = lax.axis_index("pz")
-    yy, x_lo = pts // 2, pts % 2
-    h, c = pz // 2, pz % 2
-    xt = (x_lo + h) % 2
-    g = 2 * yy + xt
-    u = 2 * i + c
-
-    tz = jnp.concatenate(
-        [lax.dynamic_slice_in_dim(jnp.asarray(part), 32 * g, 48, 0) for part in (tz_hi, tz_lo)], axis=0
-    )
-    tz = jnp.pad(tz, ((0, 32), (0, 0))).T
-    cy = jnp.concatenate([cy_hi, cy_lo], axis=0)
-    cx = jnp.concatenate([cx_hi, cx_lo], axis=0)
-
-    prof = 0.5 * lax.dynamic_slice_in_dim(jnp.pad(profile, (4, 0)), 16 * (2 * g + h), 20, 0)
-    mask = lax.dynamic_slice_in_dim(jnp.pad(well_mask, ((0, 0), (8, 0))), 32 * u, 40, 1)
-    mask = mask.astype(F32).reshape(128, 2, 8, 5).transpose(1, 3, 2, 0).reshape(2, 40, 128)
-    cz = lax.dynamic_slice_in_dim(jnp.pad(conc_start, ((0, 0), (0, 0), (4, 0))), 32 * g, 36, 2)
-    cz = cz.reshape(128, 2, 16, 36).transpose(1, 3, 2, 0)
+    tz = np.concatenate([tz_hi, tz_lo, np.zeros((8, G, 48), ml_dtypes.bfloat16)], axis=2)
+    cy = np.concatenate([cy_hi, cy_lo], axis=0)
+    cx = np.concatenate([cx_hi, cx_lo], axis=0)
 
     vmem = pl.BlockSpec(memory_space=pltpu.VMEM)
     smem = pl.BlockSpec(memory_space=pltpu.SMEM)
@@ -594,13 +695,13 @@
     total = pl.pallas_call(
         kernel,
         out_shape=jax.ShapeDtypeStruct((512, 256), F32),
-        in_specs=[smem, smem, far, far] + [vmem] * 5,
+        in_specs=[smem, smem] + [far] * 5 + [vmem] * 2,
         out_specs=vmem,
         scratch_shapes=[
             pltpu.VMEM((64, 64, 256), F32),
             pltpu.VMEM((3, 64, 64, 256), BF16),
             pltpu.VMEM((40 * 128, 128), F32),
-            pltpu.VMEM((NROUND, 4, 128, 128), F32),
+            pltpu.VMEM((NROUND, 4, 4, 32, 128), F32),
             pltpu.VMEM((NROUND, 8, 40, 256), F32),
             pltpu.VMEM((NROUND, 2, 4, 40, 256), F32),
             pltpu.VMEM((2, 20, 40, 128), F32),
@@ -615,6 +716,16 @@
             pltpu.VMEM((8, 2, 4, 16, 128), F32),
             pltpu.VMEM((4, 256, 128), F32),
             pltpu.VMEM((2, 512, 128), F32),
+            pltpu.VMEM((256, 128), BF16),
+            pltpu.VMEM((2, 4096, 128), F32),
+            pltpu.VMEM((2, 272, 128), F32),
+            pltpu.VMEM((2, 640, 128), F32),
+            pltpu.VMEM((2, 256, 128), jnp.int32),
+            pltpu.VMEM((2, 264, 128), F32),
+            pltpu.VMEM((2, 40, 128), F32),
+            dma((4, 4)),
+            dma((4, 4)),
+            dma((4,)),
             dma((NROUND, 4)),
             dma((NROUND, 4)),
             dma((NROUND,)),
@@ -624,6 +735,7 @@
             dma((4,)),
             dma((3,)),
             dma((4, 4)),
+            dma((5,)),
             dma((8,)),
             dma((8,)),
             dma((8, 2)),
@@ -632,7 +744,7 @@
         compiler_params=pltpu.CompilerParams(
             collective_id=0, has_side_effects=True, vmem_limit_bytes=60 * 2**20
         ),
-    )(point_index, prof, xi_map, basis, tz, cy, cx, cz, mask)
+    )(point_index, profile, xi_map, basis, conc_start.reshape(4096, 256), well_mask, tz, cy, cx)
     return total.reshape(32, 16, 256)
 
 

time: 89.7 us -> 90.8 us (1.012)
  Pallas kernels: 78.5 us -> 88.8 us
  local copies, waits for them, and re-layouts: 9.48 us -> 1.87 us
  other arithmetic: 1.44 us -> 0 us
    pallas_call x1, Pallas kernels: 78.5 us -> 88.8 us  [local(): pl.pallas_call(kernel, out_shape=jax.ShapeDtypeStruct((512, 256), F32), i...]
    dynamic_slice x2 -> x0, local copies, waits for them, and re-layouts: 3.95 us -> none  [the longest x1 2.88 us: local(): lax.dynamic_slice_in_dim(jnp.pad(conc_start, ((0, 0), (0, 0), (4, 0))), 3...]
    reshape x2 -> x0, local copies, waits for them, and re-layouts: 2.59 us -> none  [the longest x1 2.28 us: local(): cz = cz.reshape(128, 2, 16, 36).transpose(1, 3, 2, 0)]
    transpose x1 -> x0, local copies, waits for them, and re-layouts: 1.06 us -> none  [local(): mask.astype(F32).reshape(128, 2, 8, 5).transpose(1, 3, 2, 0)]
    unnamed x5 -> x1, local copies, waits for them, and re-layouts: 1.88 us -> 1.87 us
where the time goes in v3:
time: 90.8 us; the launch traced here: 90.7 us
  Pallas kernels  88.8 us (98%)
  local copies, waits for them, and re-layouts  1.87 us (2%)
    pallas_call x1, Pallas kernels, local(): pl.pallas_call(kernel, out_shape=jax.ShapeDtypeStruct((512, 256), F32), i...  88.8 us
    unnamed x1, local copies, waits for them, and re-layouts  1.87 us

profile of v3, /device:TPU:1, one launch (start us, length us, event | category | flops | bytes accessed | tf_op | source)
XLA Modules:
  0.0 90.7 jit_solution(11281247676923773577)
XLA Ops:
  0.0 88.8 %shard_map.91 = f32[512,256]{1,0:T(8,128)} custom-call(s32[2,3]{1,0:T(2,128)} %point.1, f32[256]{0:T(256)} %prof.1, f32[64,64,256]{2,1,0:T(8,128)} %xi_far.1, bf16[3,64,64,256]{3,2,1,0:T(8,128)(2,1)} %basis_far.1, f32[4096,256]{1,0:T(8,128)} %bitcast.2, s32[256,256]{1,0:T(8,128)} %mask_far.1, bf16[8,256,128]{2,1,0:T(8,128)(2,1)} %constant.6.clone.tz_far, ...), custom_call_target="tpu_custom_call" | custom-call | tf_op jit(solution)/shard_map/pallas_call | solution.py:695
  88.8 1.9 %copy.11 = f32[32,16,256]{2,1,0:T(8,128)} copy(f32[32,16,256]{2,1,0:T(8,128)} %bitcast.3) | data formatting | bytes 1048576

commit v4 on v3

--- a/solution.py
+++ b/solution.py
@@ -236,28 +236,31 @@
             device_id_type=MESH,
         )
 
-    turned_z[:, 0:8, :] = jnp.zeros((2, 8, 128), F32)
+    turned_z[:, 0:8, :] = jnp.zeros((8, 8, 128), F32)
     for zh in range(2):
 
         @pl.when(some_z[zh])
         def _():
             load_conc(zh).wait()
 
-    def turn_conc(y, _):
+    def turn_conc(y4, _):
+        rows = [(m, v) for m in range(4) for v in range(2)]
         for zh in range(2):
 
             @pl.when(some_z[zh])
             def _():
-                for v in range(2):
-                    turned_z[v, 4 + 128 * zh : 132 + 128 * zh, :] = start[
-                        zh, pl.ds(16 * v + y, 128, stride=32), :
+                for m, v in rows:
+                    turned_z[2 * m + v, 4 + 128 * zh : 132 + 128 * zh, :] = start[
+                        zh, pl.ds(16 * v + 4 * y4 + m, 128, stride=32), :
                     ].T
 
-        for v in range(2):
-            cz_flat[v, pl.ds(y, 40, stride=16), :] = turned_z[v, pl.ds(pl.multiple_of(32 * g, 32), 40), :]
+        for m, v in rows:
+            cz_flat[v, pl.ds(4 * y4 + m, 40, stride=16), :] = turned_z[
+                2 * m + v, pl.ds(pl.multiple_of(32 * g, 32), 40), :
+            ]
         return 0
 
-    lax.fori_loop(0, 16, turn_conc, 0)
+    lax.fori_loop(0, 4, turn_conc, 0)
 
     def turn_mask():
         turned_y[:, 0:8, :] = jnp.zeros((2, 8, 128), F32)
@@ -526,7 +529,7 @@
                 sums[v, pl.ds(16 * t + zz - 4, 8, stride=80), :] = plane[2, t, v]
 
     carry[...] = jnp.zeros(carry.shape, F32)
-    lag = 2
+    lag = 3
 
     def wait_conc():
         for core in range(2):
@@ -718,7 +721,7 @@
             pltpu.VMEM((2, 512, 128), F32),
             pltpu.VMEM((256, 128), BF16),
             pltpu.VMEM((2, 4096, 128), F32),
-            pltpu.VMEM((2, 272, 128), F32),
+            pltpu.VMEM((8, 272, 128), F32),
             pltpu.VMEM((2, 640, 128), F32),
             pltpu.VMEM((2, 256, 128), jnp.int32),
             pltpu.VMEM((2, 264, 128), F32),

time: 90.8 us -> 90.7 us (level)
  no operation moved by 1% of the time
where the time goes in v4:
time: 90.7 us; the launch traced here: 90.5 us
  Pallas kernels  88.6 us (98%)
  local copies, waits for them, and re-layouts  1.87 us (2%)
    pallas_call x1, Pallas kernels, local(): pl.pallas_call(kernel, out_shape=jax.ShapeDtypeStruct((512, 256), F32), i...  88.6 us
    unnamed x1, local copies, waits for them, and re-layouts  1.87 us

profile of v4, /device:TPU:1, one launch (start us, length us, event | category | flops | bytes accessed | tf_op | source)
XLA Modules:
  0.0 90.5 jit_solution(2006780399642159943)
XLA Ops:
  0.0 88.6 %shard_map.91 = f32[512,256]{1,0:T(8,128)} custom-call(s32[2,3]{1,0:T(2,128)} %point.1, f32[256]{0:T(256)} %prof.1, f32[64,64,256]{2,1,0:T(8,128)} %xi_far.1, bf16[3,64,64,256]{3,2,1,0:T(8,128)(2,1)} %basis_far.1, f32[4096,256]{1,0:T(8,128)} %bitcast.2, s32[256,256]{1,0:T(8,128)} %mask_far.1, bf16[8,256,128]{2,1,0:T(8,128)(2,1)} %constant.6.clone.tz_far, ...), custom_call_target="tpu_custom_call" | custom-call | tf_op jit(solution)/shard_map/pallas_call | solution.py:698
  88.6 1.9 %copy.11 = f32[32,16,256]{2,1,0:T(8,128)} copy(f32[32,16,256]{2,1,0:T(8,128)} %bitcast.3) | data formatting | bytes 1048576

commit v5 on v4

--- a/solution.py
+++ b/solution.py
@@ -15,7 +15,7 @@
 BATCH = 4
 G = 256
 NROUND = 10
-EARLY = 4
+PAIRS = 5
 ROOT3 = 1.7320508075688772
 F32 = jnp.float32
 BF16 = jnp.bfloat16
@@ -96,13 +96,10 @@
     mask,
     s0,
     r0,
-    own0,
     s1,
     r1,
-    own1,
     s2,
     r2,
-    own2,
     sc,
     rc,
     load,
@@ -323,9 +320,8 @@
                     value = xi[row] if f == 0 else basis[f - 1, row].astype(F32)
                     parts.append(value * amps[2 * part + half])
             high, low = halves(jnp.concatenate(parts, axis=0))
-            both = jnp.dot(high, tz[...], preferred_element_type=F32)
-            both += jnp.dot(low, tz[...], preferred_element_type=F32)
-            both = both.T
+            both = jnp.dot(jnp.concatenate([high, low], axis=0), tz[...], preferred_element_type=F32)
+            both = (both[0:256] + both[256:512]).T
             total = both[0:40] + both[40:80]
             for part in range(2):
                 share[pl.ds(32 * f + 2 * step + part, 40, stride=128), :] = total[
@@ -333,76 +329,61 @@
                 ]
         return 0
 
-    def stages(q, _):
-        for copy in loads(q):
-            copy.wait()
-        lax.fori_loop(4 * q, 4 * q + 4, stage, 0)
+    def stages(part, _):
+        for q in range(2):
+            for copy in loads(2 * part + q):
+                copy.wait()
+            lax.fori_loop(8 * part + 4 * q, 8 * part + 4 * q + 4, stage, 0)
         for d in (2, 3, 1):
-            early(q, d).start()
-        early_own(q).start()
+            early(part, d).start()
         return 0
 
     blocks = share.reshape(40, 4, 32, 128)
 
-    def early_parts(q, to_h, to_c):
-        rows = pl.ds(pl.multiple_of(8 * q, 8), 8)
-        src = blocks.at[pl.ds(20 * to_c + 8 * to_h, EARLY), :, rows]
-        return src, got1.at[pl.ds(0, EARLY), pz, :, rows]
-
-    def early(q, d):
+    def early(part, d):
         to_h, to_c = (h + d // 2) % 2, (c + d % 2) % 2
-        src, dst = early_parts(q, to_h, to_c)
+        rows = pl.ds(pl.multiple_of(16 * part, 16), 16)
         return pltpu.make_async_remote_copy(
-            src_ref=src,
-            dst_ref=dst,
-            send_sem=s0.at[q, d],
-            recv_sem=r0.at[q, d],
+            src_ref=blocks.at[pl.ds(20 * to_c + 8 * to_h, 2), :, rows],
+            dst_ref=got1.at[pl.ds(0, 2), pz, :, rows],
+            send_sem=s0.at[part, d],
+            recv_sem=r0.at[part, d],
             device_id=at(i, to_h, to_c),
             device_id_type=MESH,
         )
 
-    def early_own(q):
-        return pltpu.make_async_copy(*early_parts(q, h, c), own0.at[q])
-
     greet()
     load_tz.wait()
-    lax.fori_loop(0, 4, stages, 0)
-
-    def first(k, d):
+    lax.fori_loop(0, 2, stages, 0)
+
+    def first(pair, d):
         to_h, to_c = (h + d // 2) % 2, (c + d % 2) % 2
         return pltpu.make_async_remote_copy(
-            src_ref=blocks.at[20 * to_c + 8 * to_h + k],
-            dst_ref=got1.at[k, pz],
-            send_sem=s1.at[k, d],
-            recv_sem=r1.at[k, d],
+            src_ref=blocks.at[pl.ds(20 * to_c + 8 * to_h + 2 * pair, 2)],
+            dst_ref=got1.at[pl.ds(2 * pair, 2), pz],
+            send_sem=s1.at[pair, d],
+            recv_sem=r1.at[pair, d],
             device_id=at(i, to_h, to_c),
             device_id_type=MESH,
         )
 
-    def first_own(k):
-        return pltpu.make_async_copy(blocks.at[20 * c + 8 * h + k], got1.at[k, pz], own1.at[k])
-
-    def send_first(k, _):
+    def send_first(pair, _):
         for d in (2, 3, 1):
-            first(k, d).start()
-        first_own(k).start()
+            first(pair, d).start()
         return 0
 
-    lax.fori_loop(EARLY, NROUND, send_first, 0)
-
-    def second(k, d):
+    lax.fori_loop(1, PAIRS, send_first, 0)
+
+    def second(pair, d):
         to_i, to_c = (i + d // 2) % 4, (c + d % 2) % 2
         return pltpu.make_async_remote_copy(
-            src_ref=rows2.at[k, 2 * to_i + to_c],
-            dst_ref=got2.at[k, c, i],
-            send_sem=s2.at[k, d],
-            recv_sem=r2.at[k, d],
+            src_ref=rows2.at[pl.ds(2 * pair, 2), 2 * to_i + to_c],
+            dst_ref=got2.at[pl.ds(2 * pair, 2), c, i],
+            send_sem=s2.at[pair, d],
+            recv_sem=r2.at[pair, d],
             device_id=at(to_i, h, to_c),
             device_id_type=MESH,
         )
-
-    def second_own(k):
-        return pltpu.make_async_copy(rows2.at[k, u], got2.at[k, c, i], own2.at[k])
 
     lane = lax.broadcasted_iota(jnp.int32, (128, 128), 1)
     lane_low = lane < 64
@@ -411,19 +392,8 @@
     lane40 = lax.broadcasted_iota(jnp.int32, (40, 128), 1) < 64
 
     def b_contraction(k):
-        @pl.when(k == 0)
-        def _():
-            for q in range(4):
-                for d in range(1, 4):
-                    early(q, d).wait_recv()
-                early_own(q).wait()
-
-        @pl.when(k >= EARLY)
-        def _():
-            for d in range(1, 4):
-                first(k, d).wait_recv()
-            first_own(k).wait()
-
+        own = share[pl.ds(pl.multiple_of((20 * c + 8 * h + k) * 128, 128), 128), :]
+        got1[k, pz] = own.reshape(4, 32, 128)
         sides = [[], []]
         for pair in range(2):
             one, two = (got1[k, 2 * pair + m].reshape(128, 128) for m in range(2))
@@ -439,14 +409,9 @@
         total = both[0:320] + both[320:640] + rest
         for slab in range(8):
             rows2[k, slab] = total[40 * slab : 40 * slab + 40]
-        for d in (4, 5, 2, 6, 3, 7, 1):
-            second(k, d).start()
-        second_own(k).start()
+        got2[k, c, i] = rows2[k, u]
 
     def a_contraction(k):
-        for d in range(1, 8):
-            second(k, d).wait_recv()
-        second_own(k).wait()
         rows = []
         for core in range(2):
             for pair in range(2):
@@ -458,8 +423,8 @@
                     cols[1].append(jnp.where(lane40, pltpu.roll(one, 64, 1), two))
                 rows += [jnp.concatenate(col, axis=1) for col in cols]
         high, low = halves(jnp.concatenate(rows, axis=0))
-        total = jnp.dot(high, cx[0:256], preferred_element_type=F32)
-        total += jnp.dot(low, cx[0:256], preferred_element_type=F32)
+        both = jnp.dot(jnp.concatenate([high, low], axis=0), cx[0:256], preferred_element_type=F32)
+        total = both[0:320] + both[320:640]
         total += jnp.dot(high, cx[256:512], preferred_element_type=F32)
         for core in range(2):
             for f in range(4):
@@ -529,7 +494,6 @@
                 sums[v, pl.ds(16 * t + zz - 4, 8, stride=80), :] = plane[2, t, v]
 
     carry[...] = jnp.zeros(carry.shape, F32)
-    lag = 3
 
     def wait_conc():
         for core in range(2):
@@ -544,26 +508,51 @@
                 cz.at[:, pl.ds(0, 20), pl.ds(8, 8)], conc0.at[:, :, pl.ds(0, 8)], rc.at[2]
             ).wait()
 
+    def each_round(pair, work):
+        def one(sub, _):
+            work(2 * pair + sub)
+            return 0
+
+        lax.fori_loop(0, 2, one, 0)
+
+    def whole_round(k):
+        a_contraction(k)
+        for core in range(2):
+            transport(k, core, False)
+
     def rounds(step, _):
-        @pl.when(step < NROUND)
-        def _():
-            b_contraction(step)
-
-        @pl.when(step >= lag)
-        def _():
-            a_contraction(step - lag)
-
-        for early in range(2):
-
-            @pl.when(step == lag + early)
-            def _():
+        @pl.when(step == 0)
+        def _():
+            for part in range(2):
+                for d in range(1, 4):
+                    early(part, d).wait_recv()
+
+        @pl.when(jnp.logical_and(step > 0, step < PAIRS))
+        def _():
+            for d in range(1, 4):
+                first(step, d).wait_recv()
+
+        @pl.when(step < PAIRS)
+        def _():
+            each_round(step, b_contraction)
+            for d in (4, 5, 2, 6, 3, 7, 1):
+                second(step, d).start()
+
+        @pl.when(step > 0)
+        def _():
+            for d in range(1, 8):
+                second(step - 1, d).wait_recv()
+
+        @pl.when(step == 1)
+        def _():
+            for k in range(2):
+                a_contraction(k)
                 for core in range(2):
-                    transport(early, core, True)
-
-        @pl.when(step >= lag + 2)
-        def _():
-            for core in range(2):
-                transport(step - lag, core, False)
+                    transport(k, core, True)
+
+        @pl.when(step > 1)
+        def _():
+            each_round(step - 1, whole_round)
 
         return 0
 
@@ -575,7 +564,7 @@
         for r in range(4):
             row = 4 * (n % 2) + r
             nodes[n, r] = jnp.broadcast_to(listed[n // 2, row : row + 1, :], (8, 128))
-    lax.fori_loop(0, NROUND + lag, rounds, 0)
+    lax.fori_loop(0, PAIRS + 1, rounds, 0)
 
     granule = lax.broadcasted_iota(jnp.int32, (16, 128), 1) // 16
 
@@ -644,22 +633,21 @@
     for zh in range(2):
         out[:, 128 * zh : 128 * zh + 128] = final[zh]
 
-    def drain(k, _):
-        @pl.when(k >= EARLY)
+    for part in range(2):
+        for d in range(1, 4):
+            early(part, d).wait_send()
+
+    def drain(pair, _):
+        @pl.when(pair > 0)
         def _():
             for d in range(1, 4):
-                first(k, d).wait_send()
-
-        @pl.when(k < 4)
-        def _():
-            for d in range(1, 4):
-                early(k, d).wait_send()
+                first(pair, d).wait_send()
 
         for d in range(1, 8):
-            second(k, d).wait_send()
+            second(pair, d).wait_send()
         return 0
 
-    lax.fori_loop(0, NROUND, drain, 0)
+    lax.fori_loop(0, PAIRS, drain, 0)
     for dp in range(1, 8):
         node_copy(dp).wait_send()
         for half in range(2):
@@ -726,15 +714,12 @@
             pltpu.VMEM((2, 256, 128), jnp.int32),
             pltpu.VMEM((2, 264, 128), F32),
             pltpu.VMEM((2, 40, 128), F32),
-            dma((4, 4)),
-            dma((4, 4)),
-            dma((4,)),
-            dma((NROUND, 4)),
-            dma((NROUND, 4)),
-            dma((NROUND,)),
-            dma((NROUND, 8)),
-            dma((NROUND, 8)),
-            dma((NROUND,)),
+            dma((2, 4)),
+            dma((2, 4)),
+            dma((PAIRS, 4)),
+            dma((PAIRS, 4)),
+            dma((PAIRS, 8)),
+            dma((PAIRS, 8)),
             dma((4,)),
             dma((3,)),
             dma((4, 4)),

time: 90.7 us -> 87.5 us (0.965)
  Pallas kernels: 88.6 us -> 85.5 us
    pallas_call x1, Pallas kernels: 88.6 us -> 85.5 us  [local(): pl.pallas_call(kernel, out_shape=jax.ShapeDtypeStruct((512, 256), F32), i...]
where the time goes in v5:
time: 87.5 us; the launch traced here: 87.3 us
  Pallas kernels  85.5 us (98%)
  local copies, waits for them, and re-layouts  1.87 us (2%)
    pallas_call x1, Pallas kernels, local(): pl.pallas_call(kernel, out_shape=jax.ShapeDtypeStruct((512, 256), F32), i...  85.5 us
    unnamed x1, local copies, waits for them, and re-layouts  1.87 us

profile of v5, /device:TPU:1, one launch (start us, length us, event | category | flops | bytes accessed | tf_op | source)
XLA Modules:
  0.0 87.3 jit_solution(4141267107938350572)
XLA Ops:
  0.0 85.5 %shard_map.91 = f32[512,256]{1,0:T(8,128)} custom-call(s32[2,3]{1,0:T(2,128)} %point.1, f32[256]{0:T(256)} %prof.1, f32[64,64,256]{2,1,0:T(8,128)} %xi_far.1, bf16[3,64,64,256]{3,2,1,0:T(8,128)(2,1)} %basis_far.1, f32[4096,256]{1,0:T(8,128)} %bitcast.2, s32[256,256]{1,0:T(8,128)} %mask_far.1, bf16[8,256,128]{2,1,0:T(8,128)(2,1)} %constant.6.clone.tz_far, ...), custom_call_target="tpu_custom_call" | custom-call | tf_op jit(solution)/shard_map/pallas_call | solution.py:686
  85.5 1.9 %copy.11 = f32[32,16,256]{2,1,0:T(8,128)} copy(f32[32,16,256]{2,1,0:T(8,128)} %bitcast.3) | data formatting | bytes 1048576

commit v6 on v5

--- a/solution.py
+++ b/solution.py
@@ -12,7 +12,7 @@
 MESH = pl.DeviceIdType.MESH
 STEPS = 4
 POINTS = 16
-BATCH = 4
+BATCH = 2
 G = 256
 NROUND = 10
 PAIRS = 5
@@ -429,71 +429,80 @@
         for core in range(2):
             for f in range(4):
                 row = 160 * core + 40 * f
-                fields[core, f] = total[row : row + 40]
+                fields[k % 2, core, f] = total[row : row + 40]
 
     tiles = [(t, v) for t in range(5) for v in range(2)]
 
-    def transport(k, core, halo):
-        zz = 2 * k + core
-        spot_z = 16 * (2 * g + h) - 4 + zz
-        well = jnp.where(spot_z >= 0, prof[jnp.maximum(spot_z, 0)], 0.0)
-        for t, v in tiles:
-            plane[0, t, v] = conc0[v, zz, pl.ds(t, 8, stride=5), :]
-            plane[1, t, v] = mask[v, 8 * t : 8 * t + 8, :] * well
-            if not halo:
-                plane[2, t, v] = jnp.zeros((8, 128), F32)
-        steps = zz + 1 if halo else STEPS
+    def transport(k, halo):
+        sub = k % 2
+        levels = range(2)
+        for p in levels:
+            zz = 2 * k + p
+            spot_z = 16 * (2 * g + h) - 4 + zz
+            well = jnp.where(spot_z >= 0, prof[jnp.maximum(spot_z, 0)], 0.0)
+            for t, v in tiles:
+                plane[p, 0, t, v] = conc0[v, zz, pl.ds(t, 8, stride=5), :]
+                plane[p, 1, t, v] = mask[v, 8 * t : 8 * t + 8, :] * well
+                if not halo:
+                    plane[p, 2, t, v] = jnp.zeros((8, 128), F32)
 
         def some_points(group, _):
-            each = range(BATCH)
-            speed, conc = [{} for _ in each], [{} for _ in each]
-            for m in each:
+            each = [(m, p) for m in range(BATCH) for p in levels]
+            speed, conc = {e: {} for e in each}, {e: {} for e in each}
+            for m, p in each:
                 n = BATCH * group + m
                 node = [nodes[n, r] for r in range(3)]
                 for t, v in tiles:
                     logs = [
-                        fields[core, f, 8 * t : 8 * t + 8, 128 * v : 128 * v + 128] for f in range(4)
+                        fields[sub, p, f, 8 * t : 8 * t + 8, 128 * v : 128 * v + 128] for f in range(4)
                     ]
                     value = logs[0] + node[0] * logs[1] + node[1] * logs[2] + node[2] * logs[3]
-                    speed[m][t, v] = 0.125 + 0.125 * jnp.tanh(value)
-                    conc[m][t, v] = plane[0, t, v]
-            for step in range(steps):
-                last = halo and step == steps - 1
-                flux = [{tv: speed[m][tv] * conc[m][tv] for tv in tiles} for m in each]
+                    speed[m, p][t, v] = 0.125 + 0.125 * jnp.tanh(value)
+                    conc[m, p][t, v] = plane[p, 0, t, v]
+            for step in range(STEPS):
+                flux = {
+                    (m, p): {tv: speed[m, p][tv] * conc[m, p][tv] for tv in tiles}
+                    for m, p in each
+                    if not halo or step <= 2 * k + p
+                }
                 for t, v in tiles:
-                    for m in each:
+                    for m, p in each:
+                        if (m, p) not in flux:
+                            continue
                         n = BATCH * group + m
-                        here = flux[m][t, v]
-                        if last:
-                            carry[n, step, t, v] = here
+                        here = flux[m, p]
+                        more = not halo or step < 2 * k + p
+                        if more:
+                            behind = carry[n, step, t, v] if p == 0 else flux[m, 0][t, v]
+                        if p == 1:
+                            carry[n, step, t, v] = here[t, v]
+                        if not more:
                             continue
-                        behind = carry[n, step, t, v]
-                        carry[n, step, t, v] = here
-                        prev_b = flux[m][t - 1, v] if t > 0 else pltpu.roll(flux[m][4, v], 1, 0)
+                        prev_b = here[t - 1, v] if t > 0 else pltpu.roll(here[4, v], 1, 0)
                         prev_a = (
-                            flux[m][t, 0]
+                            here[t, 0]
                             if v == 1
-                            else jnp.where(lane_some, pltpu.roll(flux[m][t, 1], 1, 1), 0.0)
+                            else jnp.where(lane_some, pltpu.roll(here[t, 1], 1, 1), 0.0)
                         )
-                        conc[m][t, v] = (
-                            (conc[m][t, v] - 3.6 * here)
-                            + (plane[1, t, v] + behind)
+                        conc[m, p][t, v] = (
+                            (conc[m, p][t, v] - 3.6 * here[t, v])
+                            + (plane[p, 1, t, v] + behind)
                             + (prev_b + 1.6 * prev_a)
                         )
             if not halo:
-                for t, v in tiles:
-                    part = nodes[BATCH * group, 3] * conc[0][t, v]
-                    for m in range(1, BATCH):
-                        part += nodes[BATCH * group + m, 3] * conc[m][t, v]
-                    plane[2, t, v] += part
+                for p in levels:
+                    for t, v in tiles:
+                        part = nodes[BATCH * group, 3] * conc[0, p][t, v]
+                        for m in range(1, BATCH):
+                            part += nodes[BATCH * group + m, 3] * conc[m, p][t, v]
+                        plane[p, 2, t, v] += part
             return 0
 
         lax.fori_loop(0, POINTS // BATCH, some_points, 0)
         if not halo:
-            for t, v in tiles:
-                sums[v, pl.ds(16 * t + zz - 4, 8, stride=80), :] = plane[2, t, v]
-
-    carry[...] = jnp.zeros(carry.shape, F32)
+            for p in levels:
+                for t, v in tiles:
+                    sums[v, pl.ds(16 * t + 2 * k + p - 4, 8, stride=80), :] = plane[p, 2, t, v]
 
     def wait_conc():
         for core in range(2):
@@ -508,18 +517,6 @@
                 cz.at[:, pl.ds(0, 20), pl.ds(8, 8)], conc0.at[:, :, pl.ds(0, 8)], rc.at[2]
             ).wait()
 
-    def each_round(pair, work):
-        def one(sub, _):
-            work(2 * pair + sub)
-            return 0
-
-        lax.fori_loop(0, 2, one, 0)
-
-    def whole_round(k):
-        a_contraction(k)
-        for core in range(2):
-            transport(k, core, False)
-
     def rounds(step, _):
         @pl.when(step == 0)
         def _():
@@ -534,7 +531,8 @@
 
         @pl.when(step < PAIRS)
         def _():
-            each_round(step, b_contraction)
+            for sub in range(2):
+                b_contraction(2 * step + sub)
             for d in (4, 5, 2, 6, 3, 7, 1):
                 second(step, d).start()
 
@@ -542,17 +540,21 @@
         def _():
             for d in range(1, 8):
                 second(step - 1, d).wait_recv()
+            for sub in range(2):
+                a_contraction(2 * step - 2 + sub)
 
         @pl.when(step == 1)
         def _():
             for k in range(2):
-                a_contraction(k)
-                for core in range(2):
-                    transport(k, core, True)
+                transport(k, True)
 
         @pl.when(step > 1)
         def _():
-            each_round(step - 1, whole_round)
+            def one(sub, _):
+                transport(2 * step - 2 + sub, False)
+                return 0
+
+            lax.fori_loop(0, 2, one, 0)
 
         return 0
 
@@ -696,9 +698,9 @@
             pltpu.VMEM((NROUND, 8, 40, 256), F32),
             pltpu.VMEM((NROUND, 2, 4, 40, 256), F32),
             pltpu.VMEM((2, 20, 40, 128), F32),
-            pltpu.VMEM((2, 4, 40, 256), F32),
+            pltpu.VMEM((2, 2, 4, 40, 256), F32),
             pltpu.VMEM((POINTS, STEPS, 5, 2, 8, 128), F32),
-            pltpu.VMEM((3, 5, 2, 8, 128), F32),
+            pltpu.VMEM((2, 3, 5, 2, 8, 128), F32),
             pltpu.VMEM((64, 256), F32),
             pltpu.VMEM((8, 128), F32),
             pltpu.VMEM((8, 8, 128), F32),

time: 87.5 us -> 86 us (0.983)
  Pallas kernels: 85.5 us -> 84 us
    pallas_call x1, Pallas kernels: 85.5 us -> 84 us  [local(): pl.pallas_call(kernel, out_shape=jax.ShapeDtypeStruct((512, 256), F32), i...]
where the time goes in v6:
time: 86 us; the launch traced here: 85.9 us
  Pallas kernels  84 us (98%)
  local copies, waits for them, and re-layouts  1.87 us (2%)
    pallas_call x1, Pallas kernels, local(): pl.pallas_call(kernel, out_shape=jax.ShapeDtypeStruct((512, 256), F32), i...  84 us
    unnamed x1, local copies, waits for them, and re-layouts  1.87 us

profile of v6, /device:TPU:1, one launch (start us, length us, event | category | flops | bytes accessed | tf_op | source)
XLA Modules:
  0.0 85.9 jit_solution(13580927301476573055)
XLA Ops:
  0.0 84.0 %shard_map.91 = f32[512,256]{1,0:T(8,128)} custom-call(s32[2,3]{1,0:T(2,128)} %point.1, f32[256]{0:T(256)} %prof.1, f32[64,64,256]{2,1,0:T(8,128)} %xi_far.1, bf16[3,64,64,256]{3,2,1,0:T(8,128)(2,1)} %basis_far.1, f32[4096,256]{1,0:T(8,128)} %bitcast.2, s32[256,256]{1,0:T(8,128)} %mask_far.1, bf16[8,256,128]{2,1,0:T(8,128)(2,1)} %constant.6.clone.tz_far, ...), custom_call_target="tpu_custom_call" | custom-call | tf_op jit(solution)/shard_map/pallas_call | solution.py:688
  84.0 1.9 %copy.11 = f32[32,16,256]{2,1,0:T(8,128)} copy(f32[32,16,256]{2,1,0:T(8,128)} %bitcast.3) | data formatting | bytes 1048576

commit v7 on v6

--- a/solution.py
+++ b/solution.py
@@ -100,6 +100,8 @@
     r1,
     s2,
     r2,
+    s3,
+    r3,
     sc,
     rc,
     load,
@@ -233,13 +235,6 @@
             device_id_type=MESH,
         )
 
-    turned_z[:, 0:8, :] = jnp.zeros((8, 8, 128), F32)
-    for zh in range(2):
-
-        @pl.when(some_z[zh])
-        def _():
-            load_conc(zh).wait()
-
     def turn_conc(y4, _):
         rows = [(m, v) for m in range(4) for v in range(2)]
         for zh in range(2):
@@ -257,7 +252,15 @@
             ]
         return 0
 
-    lax.fori_loop(0, 4, turn_conc, 0)
+    def prepare_conc():
+        turned_z[:, 0:8, :] = jnp.zeros((8, 8, 128), F32)
+        for zh in range(2):
+
+            @pl.when(some_z[zh])
+            def _():
+                load_conc(zh).wait()
+
+        lax.fori_loop(0, 4, turn_conc, 0)
 
     def turn_mask():
         turned_y[:, 0:8, :] = jnp.zeros((2, 8, 128), F32)
@@ -275,6 +278,8 @@
         for dp in range(1, 8):
             node_copy(dp).start()
         listed[pts] = mine[...]
+
+    def send_conc():
         for to_h in range(2):
 
             @pl.when(slab_here(to_h))
@@ -372,7 +377,10 @@
             first(pair, d).start()
         return 0
 
-    lax.fori_loop(1, PAIRS, send_first, 0)
+    lax.fori_loop(1, 2, send_first, 0)
+    prepare_conc()
+    send_conc()
+    lax.fori_loop(2, PAIRS, send_first, 0)
 
     def second(pair, d):
         to_i, to_c = (i + d // 2) % 4, (c + d % 2) % 2
@@ -381,6 +389,18 @@
             dst_ref=got2.at[pl.ds(2 * pair, 2), c, i],
             send_sem=s2.at[pair, d],
             recv_sem=r2.at[pair, d],
+            device_id=at(to_i, h, to_c),
+            device_id_type=MESH,
+        )
+
+    def single(k, d):
+        to_i, to_c = (i + d // 2) % 4, (c + d % 2) % 2
+        slot = k % 2 + 2 * (k // 8)
+        return pltpu.make_async_remote_copy(
+            src_ref=rows2.at[k, 2 * to_i + to_c],
+            dst_ref=got2.at[k, c, i],
+            send_sem=s3.at[slot, d],
+            recv_sem=r3.at[slot, d],
             device_id=at(to_i, h, to_c),
             device_id_type=MESH,
         )
@@ -517,6 +537,70 @@
                 cz.at[:, pl.ds(0, 20), pl.ds(8, 8)], conc0.at[:, :, pl.ds(0, 8)], rc.at[2]
             ).wait()
 
+    granule = lax.broadcasted_iota(jnp.int32, (8, 128), 1) // 16
+    zr = 16 * (4 * yy + 2 * xt + h)
+
+    def home(zp, dp, half):
+        to = (pts + dp) % 8
+        return pltpu.make_async_remote_copy(
+            src_ref=parcel.at[zp, to, half],
+            dst_ref=landed.at[:, pl.ds(pl.multiple_of(zr + 8 * zp, 8), 8)],
+            send_sem=so.at[zp, dp, half],
+            recv_sem=ro.at[zp, dp, h],
+            device_id={"pts": to, "py": i, "pz": 2 * c + half},
+            device_id_type=MESH,
+        )
+
+    def home_own(zp, half):
+        return pltpu.make_async_copy(
+            parcel.at[zp, pts, half],
+            landed.at[:, pl.ds(pl.multiple_of(zr + 8 * zp, 8), 8)],
+            ro.at[zp, 0, h],
+        )
+
+    def go_home(zp):
+        def regroup(which, _):
+            half, yg = which // 4, which % 4
+            arrays = []
+            for y in range(4):
+                for v in range(2):
+                    row = pl.multiple_of(16 * (8 + 16 * half + 4 * yg + y) + 8 * zp, 8)
+                    arrays.append(sums[v, pl.ds(row, 8), :])
+            for bit in (4, 2, 1):
+                clear = (granule // bit) % 2 == 0
+                for m in range(8):
+                    if m // bit % 2 == 0:
+                        one, two = arrays[m], arrays[m + bit]
+                        arrays[m] = jnp.where(clear, one, pltpu.roll(two, 16 * bit, 1))
+                        arrays[m + bit] = jnp.where(clear, pltpu.roll(one, 128 - 16 * bit, 1), two)
+            for p in range(8):
+                parcel[zp, p, half, yg] = arrays[p]
+            return 0
+
+        for half in range(2):
+            lax.fori_loop(4 * half, 4 * half + 4, regroup, 0)
+            here = jnp.logical_and(c == h, c == half)
+
+            @pl.when(here)
+            def _():
+                home_own(zp, half).start()
+
+            @pl.when(jnp.logical_not(here))
+            def _():
+                home(zp, 0, half).start()
+
+            for dp in range(1, 8):
+                home(zp, dp, half).start()
+
+    def prepare_rest():
+        turn_mask()
+        for dp in range(1, 8):
+            node_copy(dp).wait_recv()
+        for n in range(POINTS):
+            for r in range(4):
+                row = 4 * (n % 2) + r
+                nodes[n, r] = jnp.broadcast_to(listed[n // 2, row : row + 1, :], (8, 128))
+
     def rounds(step, _):
         @pl.when(step == 0)
         def _():
@@ -529,101 +613,75 @@
             for d in range(1, 4):
                 first(step, d).wait_recv()
 
-        @pl.when(step < PAIRS)
+        @pl.when(jnp.logical_or(step == 0, step == PAIRS - 1))
+        def _():
+            def one(k, _):
+                b_contraction(k)
+                for d in (4, 5, 2, 6, 3, 7, 1):
+                    single(k, d).start()
+                return 0
+
+            lax.fori_loop(2 * step, 2 * step + 2, one, 0)
+
+        @pl.when(step == 0)
+        def _():
+            prepare_rest()
+
+        @pl.when(jnp.logical_and(step > 0, step < PAIRS - 1))
         def _():
             for sub in range(2):
                 b_contraction(2 * step + sub)
             for d in (4, 5, 2, 6, 3, 7, 1):
                 second(step, d).start()
 
-        @pl.when(step > 0)
+        @pl.when(step == 1)
+        def _():
+            wait_conc()
+            for k in range(2):
+                for d in range(1, 8):
+                    single(k, d).wait_recv()
+                a_contraction(k)
+                transport(k, True)
+
+        @pl.when(jnp.logical_and(step > 1, step < PAIRS))
         def _():
             for d in range(1, 8):
                 second(step - 1, d).wait_recv()
             for sub in range(2):
                 a_contraction(2 * step - 2 + sub)
 
-        @pl.when(step == 1)
-        def _():
-            for k in range(2):
-                transport(k, True)
-
-        @pl.when(step > 1)
-        def _():
             def one(sub, _):
                 transport(2 * step - 2 + sub, False)
                 return 0
 
             lax.fori_loop(0, 2, one, 0)
 
+        @pl.when(step == 3)
+        def _():
+            go_home(0)
+
+        @pl.when(step == PAIRS)
+        def _():
+            def one(k, _):
+                for d in range(1, 8):
+                    single(k, d).wait_recv()
+                a_contraction(k)
+                transport(k, False)
+                return 0
+
+            lax.fori_loop(2 * PAIRS - 2, 2 * PAIRS, one, 0)
+
         return 0
 
-    turn_mask()
-    wait_conc()
-    for dp in range(1, 8):
-        node_copy(dp).wait_recv()
-    for n in range(POINTS):
-        for r in range(4):
-            row = 4 * (n % 2) + r
-            nodes[n, r] = jnp.broadcast_to(listed[n // 2, row : row + 1, :], (8, 128))
     lax.fori_loop(0, PAIRS + 1, rounds, 0)
 
-    granule = lax.broadcasted_iota(jnp.int32, (16, 128), 1) // 16
-
-    def regroup(which, _):
-        half, yg = which // 4, which % 4
-        arrays = []
-        for yy in range(4):
-            for v in range(2):
-                row = pl.multiple_of(16 * (8 + 16 * half + 4 * yg + yy), 16)
-                arrays.append(sums[v, pl.ds(row, 16), :])
-        for bit in (4, 2, 1):
-            clear = (granule // bit) % 2 == 0
-            for m in range(8):
-                if m // bit % 2 == 0:
-                    one, two = arrays[m], arrays[m + bit]
-                    arrays[m] = jnp.where(clear, one, pltpu.roll(two, 16 * bit, 1))
-                    arrays[m + bit] = jnp.where(clear, pltpu.roll(one, 128 - 16 * bit, 1), two)
-        for p in range(8):
-            parcel[p, half, yg] = arrays[p]
-        return 0
-
-    zr = pl.multiple_of(16 * (4 * yy + 2 * xt + h), 16)
-
-    def home(dp, half):
-        to = (pts + dp) % 8
-        return pltpu.make_async_remote_copy(
-            src_ref=parcel.at[to, half],
-            dst_ref=landed.at[:, pl.ds(zr, 16)],
-            send_sem=so.at[dp, half],
-            recv_sem=ro.at[dp, h],
-            device_id={"pts": to, "py": i, "pz": 2 * c + half},
-            device_id_type=MESH,
-        )
-
-    def home_own(half):
-        return pltpu.make_async_copy(parcel.at[pts, half], landed.at[:, pl.ds(zr, 16)], ro.at[0, h])
-
-    for half in range(2):
-        lax.fori_loop(4 * half, 4 * half + 4, regroup, 0)
-        here = jnp.logical_and(c == h, c == half)
-
-        @pl.when(here)
-        def _():
-            home_own(half).start()
-
-        @pl.when(jnp.logical_not(here))
-        def _():
-            home(0, half).start()
-
-        for dp in range(1, 8):
-            home(dp, half).start()
-
-    for dp in range(8):
-        for from_h in range(2):
-            pltpu.make_async_copy(
-                parcel.at[0, 0], landed.at[:, pl.ds(0, 16)], ro.at[dp, from_h]
-            ).wait()
+    go_home(1)
+    for zp in range(2):
+        for dp in range(8):
+            for from_h in range(2):
+                pltpu.make_async_copy(
+                    parcel.at[0, 0, 0], landed.at[:, pl.ds(0, 8)], ro.at[zp, dp, from_h]
+                ).wait()
 
     for yg in range(4):
         for zh in range(2):
@@ -640,25 +698,32 @@
             early(part, d).wait_send()
 
     def drain(pair, _):
-        @pl.when(pair > 0)
-        def _():
-            for d in range(1, 4):
-                first(pair, d).wait_send()
-
+        for d in range(1, 4):
+            first(pair, d).wait_send()
+        return 0
+
+    lax.fori_loop(1, PAIRS, drain, 0)
+
+    def drain_pairs(pair, _):
         for d in range(1, 8):
             second(pair, d).wait_send()
         return 0
 
-    lax.fori_loop(0, PAIRS, drain, 0)
+    lax.fori_loop(1, PAIRS - 1, drain_pairs, 0)
+    for k in (0, 1, 8, 9):
+        for d in range(1, 8):
+            single(k, d).wait_send()
     for dp in range(1, 8):
         node_copy(dp).wait_send()
-        for half in range(2):
-            home(dp, half).wait_send()
+        for zp in range(2):
+            for half in range(2):
+                home(zp, dp, half).wait_send()
     for half in range(2):
 
         @pl.when(jnp.logical_not(jnp.logical_and(c == h, c == half)))
         def _():
-            home(0, half).wait_send()
+            for zp in range(2):
+                home(zp, 0, half).wait_send()
 
     for to_h in range(2):
 
@@ -706,7 +771,7 @@
             pltpu.VMEM((8, 8, 128), F32),
             pltpu.VMEM((POINTS, 4, 8, 128), F32),
             pltpu.VMEM((2, 640, 128), F32),
-            pltpu.VMEM((8, 2, 4, 16, 128), F32),
+            pltpu.VMEM((2, 8, 2, 4, 8, 128), F32),
             pltpu.VMEM((4, 256, 128), F32),
             pltpu.VMEM((2, 512, 128), F32),
             pltpu.VMEM((256, 128), BF16),
@@ -722,14 +787,16 @@
             dma((PAIRS, 4)),
             dma((PAIRS, 8)),
             dma((PAIRS, 8)),
+            dma((4, 8)),
+            dma((4, 8)),
             dma((4,)),
             dma((3,)),
             dma((4, 4)),
             dma((5,)),
             dma((8,)),
             dma((8,)),
-            dma((8, 2)),
-            dma((8, 2)),
+            dma((2, 8, 2)),
+            dma((2, 8, 2)),
         ],
         compiler_params=pltpu.CompilerParams(
             collective_id=0, has_side_effects=True, vmem_limit_bytes=60 * 2**20

time: 86 us -> 87.4 us (1.016)
  Pallas kernels: 84 us -> 85.3 us
    pallas_call x1, Pallas kernels: 84 us -> 85.3 us  [local(): pl.pallas_call(kernel, out_shape=jax.ShapeDtypeStruct((512, 256), F32), i...]
where the time goes in v7:
time: 87.4 us; the launch traced here: 87.2 us
  Pallas kernels  85.3 us (98%)
  local copies, waits for them, and re-layouts  1.87 us (2%)
    pallas_call x1, Pallas kernels, local(): pl.pallas_call(kernel, out_shape=jax.ShapeDtypeStruct((512, 256), F32), i...  85.3 us
    unnamed x1, local copies, waits for them, and re-layouts  1.87 us

profile of v7, /device:TPU:1, one launch (start us, length us, event | category | flops | bytes accessed | tf_op | source)
XLA Modules:
  0.0 87.2 jit_solution(13162485674713661024)
XLA Ops:
  0.0 85.3 %shard_map.91 = f32[512,256]{1,0:T(8,128)} custom-call(s32[2,3]{1,0:T(2,128)} %point.1, f32[256]{0:T(256)} %prof.1, f32[64,64,256]{2,1,0:T(8,128)} %xi_far.1, bf16[3,64,64,256]{3,2,1,0:T(8,128)(2,1)} %basis_far.1, f32[4096,256]{1,0:T(8,128)} %bitcast.2, s32[256,256]{1,0:T(8,128)} %mask_far.1, bf16[8,256,128]{2,1,0:T(8,128)(2,1)} %constant.6.clone.tz_far, ...), custom_call_target="tpu_custom_call" | custom-call | tf_op jit(solution)/shard_map/pallas_call | solution.py:753
  85.3 1.9 %copy.11 = f32[32,16,256]{2,1,0:T(8,128)} copy(f32[32,16,256]{2,1,0:T(8,128)} %bitcast.3) | data formatting | bytes 1048576

commit v8 on v6

--- a/solution.py
+++ b/solution.py
@@ -139,7 +139,7 @@
     def loads(q):
         copies = []
         for half in range(2):
-            rows = pl.ds(pl.multiple_of(8 * q + 32 * half, 8), 8)
+            rows = pl.ds(pl.multiple_of(16 * q + 32 * half, 16), 16)
             copies.append(pltpu.make_async_copy(xi_far.at[rows], xi.at[rows], load.at[q, 2 * half]))
             copies.append(
                 pltpu.make_async_copy(basis_far.at[:, rows], basis.at[:, rows], load.at[q, 2 * half + 1])
@@ -170,7 +170,7 @@
             load_conc(zh).start()
 
     load_tz.start()
-    lax.fori_loop(0, 4, start_loads, 0)
+    lax.fori_loop(0, 2, start_loads, 0)
     for yh in range(2):
         load_mask(yh).start()
 
@@ -330,10 +330,9 @@
         return 0
 
     def stages(part, _):
-        for q in range(2):
-            for copy in loads(2 * part + q):
-                copy.wait()
-            lax.fori_loop(8 * part + 4 * q, 8 * part + 4 * q + 4, stage, 0)
+        for copy in loads(part):
+            copy.wait()
+        lax.fori_loop(8 * part, 8 * part + 8, stage, 0)
         for d in (2, 3, 1):
             early(part, d).start()
         return 0
@@ -359,8 +358,8 @@
     def first(pair, d):
         to_h, to_c = (h + d // 2) % 2, (c + d % 2) % 2
         return pltpu.make_async_remote_copy(
-            src_ref=blocks.at[pl.ds(20 * to_c + 8 * to_h + 2 * pair, 2)],
-            dst_ref=got1.at[pl.ds(2 * pair, 2), pz],
+            src_ref=blocks.at[pl.ds(20 * to_c + 8 * to_h + 4 * pair - 2, 4)],
+            dst_ref=got1.at[pl.ds(4 * pair - 2, 4), pz],
             send_sem=s1.at[pair, d],
             recv_sem=r1.at[pair, d],
             device_id=at(i, to_h, to_c),
@@ -372,7 +371,7 @@
             first(pair, d).start()
         return 0
 
-    lax.fori_loop(1, PAIRS, send_first, 0)
+    lax.fori_loop(1, 3, send_first, 0)
 
     def second(pair, d):
         to_i, to_c = (i + d // 2) % 4, (c + d % 2) % 2
@@ -388,7 +387,7 @@
     lane = lax.broadcasted_iota(jnp.int32, (128, 128), 1)
     lane_low = lane < 64
     lane8 = lax.broadcasted_iota(jnp.int32, (8, 128), 1)
-    lane_some = lane8 > 0
+    edge = jnp.where(lane8 > 0, 1.6 * 1.6, 0.0).astype(F32)
     lane40 = lax.broadcasted_iota(jnp.int32, (40, 128), 1) < 64
 
     def b_contraction(k):
@@ -441,8 +440,9 @@
             spot_z = 16 * (2 * g + h) - 4 + zz
             well = jnp.where(spot_z >= 0, prof[jnp.maximum(spot_z, 0)], 0.0)
             for t, v in tiles:
-                plane[p, 0, t, v] = conc0[v, zz, pl.ds(t, 8, stride=5), :]
-                plane[p, 1, t, v] = mask[v, 8 * t : 8 * t + 8, :] * well
+                share_v = 1.0 if v == 0 else 1.0 / 1.6
+                plane[p, 0, t, v] = conc0[v, zz, pl.ds(t, 8, stride=5), :] * share_v
+                plane[p, 1, t, v] = mask[v, 8 * t : 8 * t + 8, :] * (well * share_v)
                 if not halo:
                     plane[p, 2, t, v] = jnp.zeros((8, 128), F32)
 
@@ -479,15 +479,11 @@
                         if not more:
                             continue
                         prev_b = here[t - 1, v] if t > 0 else pltpu.roll(here[4, v], 1, 0)
-                        prev_a = (
-                            here[t, 0]
-                            if v == 1
-                            else jnp.where(lane_some, pltpu.roll(here[t, 1], 1, 1), 0.0)
-                        )
+                        prev_a = here[t, 0] if v == 1 else edge * pltpu.roll(here[t, 1], 1, 1)
                         conc[m, p][t, v] = (
                             (conc[m, p][t, v] - 3.6 * here[t, v])
                             + (plane[p, 1, t, v] + behind)
-                            + (prev_b + 1.6 * prev_a)
+                            + (prev_b + prev_a)
                         )
             if not halo:
                 for p in levels:
@@ -502,7 +498,9 @@
         if not halo:
             for p in levels:
                 for t, v in tiles:
-                    sums[v, pl.ds(16 * t + 2 * k + p - 4, 8, stride=80), :] = plane[p, 2, t, v]
+                    sums[v, pl.ds(16 * t + 2 * k + p - 4, 8, stride=80), :] = (
+                        plane[p, 2, t, v] * (1.0 if v == 0 else 1.6)
+                    )
 
     def wait_conc():
         for core in range(2):
@@ -524,10 +522,10 @@
                 for d in range(1, 4):
                     early(part, d).wait_recv()
 
-        @pl.when(jnp.logical_and(step > 0, step < PAIRS))
+        @pl.when(jnp.logical_or(step == 1, step == 3))
         def _():
             for d in range(1, 4):
-                first(step, d).wait_recv()
+                first((step + 1) // 2, d).wait_recv()
 
         @pl.when(step < PAIRS)
         def _():
@@ -640,7 +638,7 @@
             early(part, d).wait_send()
 
     def drain(pair, _):
-        @pl.when(pair > 0)
+        @pl.when(jnp.logical_and(pair > 0, pair < 3))
         def _():
             for d in range(1, 4):
                 first(pair, d).wait_send()

time: 86 us -> 91.2 us (1.060)
  Pallas kernels: 84 us -> 89.2 us
    pallas_call x1, Pallas kernels: 84 us -> 89.2 us  [local(): pl.pallas_call(kernel, out_shape=jax.ShapeDtypeStruct((512, 256), F32), i...]
where the time goes in v8:
time: 91.2 us; the launch traced here: 91 us
  Pallas kernels  89.2 us (98%)
  local copies, waits for them, and re-layouts  1.87 us (2%)
    pallas_call x1, Pallas kernels, local(): pl.pallas_call(kernel, out_shape=jax.ShapeDtypeStruct((512, 256), F32), i...  89.2 us
    unnamed x1, local copies, waits for them, and re-layouts  1.87 us

profile of v8, /device:TPU:1, one launch (start us, length us, event | category | flops | bytes accessed | tf_op | source)
XLA Modules:
  0.0 91.0 jit_solution(7045873948309802370)
XLA Ops:
  0.0 89.2 %shard_map.91 = f32[512,256]{1,0:T(8,128)} custom-call(s32[2,3]{1,0:T(2,128)} %point.1, f32[256]{0:T(256)} %prof.1, f32[64,64,256]{2,1,0:T(8,128)} %xi_far.1, bf16[3,64,64,256]{3,2,1,0:T(8,128)(2,1)} %basis_far.1, f32[4096,256]{1,0:T(8,128)} %bitcast.2, s32[256,256]{1,0:T(8,128)} %mask_far.1, bf16[8,256,128]{2,1,0:T(8,128)(2,1)} %constant.6.clone.tz_far, ...), custom_call_target="tpu_custom_call" | custom-call | tf_op jit(solution)/shard_map/pallas_call | solution.py:686
  89.2 1.9 %copy.11 = f32[32,16,256]{2,1,0:T(8,128)} copy(f32[32,16,256]{2,1,0:T(8,128)} %bitcast.3) | data formatting | bytes 1048576

commit v9 on v8

--- a/solution.py
+++ b/solution.py
@@ -94,7 +94,6 @@
     wells,
     turned_y,
     mask,
-    s0,
     r0,
     s1,
     r1,
@@ -105,7 +104,6 @@
     load,
     prep,
     sn,
-    rn,
     so,
     ro,
 ):
@@ -121,6 +119,9 @@
 
     def at(i_, h_, c_):
         return {"pts": 2 * yy + (xt + h_) % 2, "py": i_, "pz": 2 * h_ + c_}
+
+    def await_bytes(view, sem):
+        pltpu.make_async_copy(view, view, sem).wait()
 
     barrier = pltpu.get_barrier_semaphore()
     peers = []
@@ -139,10 +140,10 @@
     def loads(q):
         copies = []
         for half in range(2):
-            rows = pl.ds(pl.multiple_of(16 * q + 32 * half, 16), 16)
-            copies.append(pltpu.make_async_copy(xi_far.at[rows], xi.at[rows], load.at[q, 2 * half]))
+            rows = pl.ds(pl.multiple_of(8 * q + 32 * half, 8), 8)
+            copies.append(pltpu.make_async_copy(xi_far.at[rows], xi.at[rows], load.at[q, 0]))
             copies.append(
-                pltpu.make_async_copy(basis_far.at[:, rows], basis.at[:, rows], load.at[q, 2 * half + 1])
+                pltpu.make_async_copy(basis_far.at[:, rows], basis.at[:, rows], load.at[q, 1])
             )
         return copies
 
@@ -170,7 +171,7 @@
             load_conc(zh).start()
 
     load_tz.start()
-    lax.fori_loop(0, 2, start_loads, 0)
+    lax.fori_loop(0, 4, start_loads, 0)
     for yh in range(2):
         load_mask(yh).start()
 
@@ -227,8 +228,8 @@
         return pltpu.make_async_remote_copy(
             src_ref=mine,
             dst_ref=listed.at[pts],
-            send_sem=sn.at[dp],
-            recv_sem=rn.at[dp],
+            send_sem=sn.at[0],
+            recv_sem=sn.at[1],
             device_id={"pts": (pts + dp) % 8, "py": i, "pz": pz},
             device_id_type=MESH,
         )
@@ -330,25 +331,41 @@
         return 0
 
     def stages(part, _):
-        for copy in loads(part):
-            copy.wait()
-        lax.fori_loop(8 * part, 8 * part + 8, stage, 0)
-        for d in (2, 3, 1):
-            early(part, d).start()
+        for q in range(2):
+            await_bytes(xi.at[pl.ds(0, 16)], load.at[2 * part + q, 0])
+            await_bytes(basis.at[:, pl.ds(0, 16)], load.at[2 * part + q, 1])
+            lax.fori_loop(8 * part + 4 * q, 8 * part + 4 * q + 4, stage, 0)
+
+        @pl.when(part == 0)
+        def _():
+            for d in (2, 3, 1):
+                early(0, 0, 4, d).start()
+
+        @pl.when(part == 1)
+        def _():
+            for begin in (0, 2):
+                for d in (2, 3, 1):
+                    early(1, begin, 2, d).start()
+
         return 0
 
     blocks = share.reshape(40, 4, 32, 128)
 
-    def early(part, d):
+    def early(part, begin, count, d):
         to_h, to_c = (h + d // 2) % 2, (c + d % 2) % 2
-        rows = pl.ds(pl.multiple_of(16 * part, 16), 16)
+        rows = pl.ds(16 * part, 16)
         return pltpu.make_async_remote_copy(
-            src_ref=blocks.at[pl.ds(20 * to_c + 8 * to_h, 2), :, rows],
-            dst_ref=got1.at[pl.ds(0, 2), pz, :, rows],
-            send_sem=s0.at[part, d],
-            recv_sem=r0.at[part, d],
+            src_ref=blocks.at[pl.ds(20 * to_c + 8 * to_h + begin, count), :, rows],
+            dst_ref=got1.at[pl.ds(begin, count), pz, :, rows],
+            send_sem=s1.at[0],
+            recv_sem=r0.at[part + begin // 2],
             device_id=at(i, to_h, to_c),
             device_id_type=MESH,
+        )
+
+    def early_come(part, begin, count):
+        await_bytes(
+            got1.at[pl.ds(begin, count), pl.ds(0, 3), :, pl.ds(16 * part, 16)], r0.at[part + begin // 2]
         )
 
     greet()
@@ -358,10 +375,10 @@
     def first(pair, d):
         to_h, to_c = (h + d // 2) % 2, (c + d % 2) % 2
         return pltpu.make_async_remote_copy(
-            src_ref=blocks.at[pl.ds(20 * to_c + 8 * to_h + 4 * pair - 2, 4)],
-            dst_ref=got1.at[pl.ds(4 * pair - 2, 4), pz],
-            send_sem=s1.at[pair, d],
-            recv_sem=r1.at[pair, d],
+            src_ref=blocks.at[pl.ds(20 * to_c + 8 * to_h + 2 * pair, 2)],
+            dst_ref=got1.at[pl.ds(2 * pair, 2), pz],
+            send_sem=s1.at[0],
+            recv_sem=r1.at[pair],
             device_id=at(i, to_h, to_c),
             device_id_type=MESH,
         )
@@ -371,15 +388,15 @@
             first(pair, d).start()
         return 0
 
-    lax.fori_loop(1, 3, send_first, 0)
+    lax.fori_loop(2, PAIRS, send_first, 0)
 
     def second(pair, d):
         to_i, to_c = (i + d // 2) % 4, (c + d % 2) % 2
         return pltpu.make_async_remote_copy(
             src_ref=rows2.at[pl.ds(2 * pair, 2), 2 * to_i + to_c],
-            dst_ref=got2.at[pl.ds(2 * pair, 2), c, i],
-            send_sem=s2.at[pair, d],
-            recv_sem=r2.at[pair, d],
+            dst_ref=got2.at[pl.ds(2 * pair, 2), 4 * c + i],
+            send_sem=s2.at[0],
+            recv_sem=r2.at[pair],
             device_id=at(to_i, h, to_c),
             device_id_type=MESH,
         )
@@ -408,7 +425,7 @@
         total = both[0:320] + both[320:640] + rest
         for slab in range(8):
             rows2[k, slab] = total[40 * slab : 40 * slab + 40]
-        got2[k, c, i] = rows2[k, u]
+        got2[k, 4 * c + i] = rows2[k, u]
 
     def a_contraction(k):
         rows = []
@@ -416,8 +433,8 @@
             for pair in range(2):
                 cols = [[], []]
                 for group in range(2):
-                    one = got2[k, core, 2 * group, :, 128 * pair : 128 * pair + 128]
-                    two = got2[k, core, 2 * group + 1, :, 128 * pair : 128 * pair + 128]
+                    one = got2[k, 4 * core + 2 * group, :, 128 * pair : 128 * pair + 128]
+                    two = got2[k, 4 * core + 2 * group + 1, :, 128 * pair : 128 * pair + 128]
                     cols[0].append(jnp.where(lane40, one, pltpu.roll(two, 64, 1)))
                     cols[1].append(jnp.where(lane40, pltpu.roll(one, 64, 1), two))
                 rows += [jnp.concatenate(col, axis=1) for col in cols]
@@ -518,14 +535,16 @@
     def rounds(step, _):
         @pl.when(step == 0)
         def _():
-            for part in range(2):
-                for d in range(1, 4):
-                    early(part, d).wait_recv()
-
-        @pl.when(jnp.logical_or(step == 1, step == 3))
-        def _():
-            for d in range(1, 4):
-                first((step + 1) // 2, d).wait_recv()
+            early_come(0, 0, 4)
+            early_come(1, 0, 2)
+
+        @pl.when(step == 1)
+        def _():
+            early_come(1, 2, 2)
+
+        @pl.when(jnp.logical_and(step > 1, step < PAIRS))
+        def _():
+            await_bytes(got1.at[pl.ds(2 * step, 2), pl.ds(0, 3)], r1.at[step])
 
         @pl.when(step < PAIRS)
         def _():
@@ -536,8 +555,7 @@
 
         @pl.when(step > 0)
         def _():
-            for d in range(1, 8):
-                second(step - 1, d).wait_recv()
+            await_bytes(got2.at[pl.ds(2 * step - 2, 2), pl.ds(0, 7)], r2.at[step - 1])
             for sub in range(2):
                 a_contraction(2 * step - 2 + sub)
 
@@ -558,8 +576,7 @@
 
     turn_mask()
     wait_conc()
-    for dp in range(1, 8):
-        node_copy(dp).wait_recv()
+    await_bytes(listed.at[pl.ds(0, 7)], sn.at[1])
     for n in range(POINTS):
         for r in range(4):
             row = 4 * (n % 2) + r
@@ -593,14 +610,14 @@
         return pltpu.make_async_remote_copy(
             src_ref=parcel.at[to, half],
             dst_ref=landed.at[:, pl.ds(zr, 16)],
-            send_sem=so.at[dp, half],
-            recv_sem=ro.at[dp, h],
+            send_sem=so.at[0 if dp else 1 + half],
+            recv_sem=ro.at[0],
             device_id={"pts": to, "py": i, "pz": 2 * c + half},
             device_id_type=MESH,
         )
 
     def home_own(half):
-        return pltpu.make_async_copy(parcel.at[pts, half], landed.at[:, pl.ds(zr, 16)], ro.at[0, h])
+        return pltpu.make_async_copy(parcel.at[pts, half], landed.at[:, pl.ds(zr, 16)], ro.at[0])
 
     for half in range(2):
         lax.fori_loop(4 * half, 4 * half + 4, regroup, 0)
@@ -617,11 +634,7 @@
         for dp in range(1, 8):
             home(dp, half).start()
 
-    for dp in range(8):
-        for from_h in range(2):
-            pltpu.make_async_copy(
-                parcel.at[0, 0], landed.at[:, pl.ds(0, 16)], ro.at[dp, from_h]
-            ).wait()
+    await_bytes(landed, ro.at[0])
 
     for yg in range(4):
         for zh in range(2):
@@ -633,25 +646,10 @@
     for zh in range(2):
         out[:, 128 * zh : 128 * zh + 128] = final[zh]
 
-    for part in range(2):
-        for d in range(1, 4):
-            early(part, d).wait_send()
-
-    def drain(pair, _):
-        @pl.when(jnp.logical_and(pair > 0, pair < 3))
-        def _():
-            for d in range(1, 4):
-                first(pair, d).wait_send()
-
-        for d in range(1, 8):
-            second(pair, d).wait_send()
-        return 0
-
-    lax.fori_loop(0, PAIRS, drain, 0)
-    for dp in range(1, 8):
-        node_copy(dp).wait_send()
-        for half in range(2):
-            home(dp, half).wait_send()
+    await_bytes(share.at[pl.ds(0, 3 * 128 * NROUND)], s1.at[0])
+    await_bytes(rows2.at[:, pl.ds(0, 7)], s2.at[0])
+    await_bytes(listed.at[pl.ds(0, 7)], sn.at[0])
+    await_bytes(parcel.at[pl.ds(0, 7)], so.at[0])
     for half in range(2):
 
         @pl.when(jnp.logical_not(jnp.logical_and(c == h, c == half)))
@@ -694,7 +692,7 @@
             pltpu.VMEM((40 * 128, 128), F32),
             pltpu.VMEM((NROUND, 4, 4, 32, 128), F32),
             pltpu.VMEM((NROUND, 8, 40, 256), F32),
-            pltpu.VMEM((NROUND, 2, 4, 40, 256), F32),
+            pltpu.VMEM((NROUND, 8, 40, 256), F32),
             pltpu.VMEM((2, 20, 40, 128), F32),
             pltpu.VMEM((2, 2, 4, 40, 256), F32),
             pltpu.VMEM((POINTS, STEPS, 5, 2, 8, 128), F32),
@@ -714,20 +712,18 @@
             pltpu.VMEM((2, 256, 128), jnp.int32),
             pltpu.VMEM((2, 264, 128), F32),
             pltpu.VMEM((2, 40, 128), F32),
-            dma((2, 4)),
-            dma((2, 4)),
-            dma((PAIRS, 4)),
-            dma((PAIRS, 4)),
-            dma((PAIRS, 8)),
-            dma((PAIRS, 8)),
+            dma((3,)),
+            dma((1,)),
+            dma((PAIRS,)),
+            dma((1,)),
+            dma((PAIRS,)),
             dma((4,)),
             dma((3,)),
-            dma((4, 4)),
+            dma((4, 2)),
             dma((5,)),
-            dma((8,)),
-            dma((8,)),
-            dma((8, 2)),
-            dma((8, 2)),
+            dma((2,)),
+            dma((3,)),
+            dma((1,)),
         ],
         compiler_params=pltpu.CompilerParams(
             collective_id=0, has_side_effects=True, vmem_limit_bytes=60 * 2**20

time: 91.2 us -> 87.3 us (0.957)
  Pallas kernels: 89.2 us -> 85.2 us
    pallas_call x1, Pallas kernels: 89.2 us -> 85.2 us  [local(): pl.pallas_call(kernel, out_shape=jax.ShapeDtypeStruct((512, 256), F32), i...]
where the time goes in v9:
time: 87.3 us; the launch traced here: 87.1 us
  Pallas kernels  85.2 us (98%)
  local copies, waits for them, and re-layouts  1.87 us (2%)
    pallas_call x1, Pallas kernels, local(): pl.pallas_call(kernel, out_shape=jax.ShapeDtypeStruct((512, 256), F32), i...  85.2 us
    unnamed x1, local copies, waits for them, and re-layouts  1.87 us

profile of v9, /device:TPU:1, one launch (start us, length us, event | category | flops | bytes accessed | tf_op | source)
XLA Modules:
  0.0 87.1 jit_solution(5406410831050099145)
XLA Ops:
  0.0 85.2 %shard_map.91 = f32[512,256]{1,0:T(8,128)} custom-call(s32[2,3]{1,0:T(2,128)} %point.1, f32[256]{0:T(256)} %prof.1, f32[64,64,256]{2,1,0:T(8,128)} %xi_far.1, bf16[3,64,64,256]{3,2,1,0:T(8,128)(2,1)} %basis_far.1, f32[4096,256]{1,0:T(8,128)} %bitcast.2, s32[256,256]{1,0:T(8,128)} %mask_far.1, bf16[8,256,128]{2,1,0:T(8,128)(2,1)} %constant.6.clone.tz_far, ...), custom_call_target="tpu_custom_call" | custom-call | tf_op jit(solution)/shard_map/pallas_call | solution.py:684
  85.2 1.9 %copy.11 = f32[32,16,256]{2,1,0:T(8,128)} copy(f32[32,16,256]{2,1,0:T(8,128)} %bitcast.3) | data formatting | bytes 1048576

commit v10 on v9

--- a/solution.py
+++ b/solution.py
@@ -99,6 +99,7 @@
     r1,
     s2,
     r2,
+    r3,
     sc,
     rc,
     load,
@@ -339,13 +340,13 @@
         @pl.when(part == 0)
         def _():
             for d in (2, 3, 1):
-                early(0, 0, 4, d).start()
+                early(0, 0, 2, d).start()
 
         @pl.when(part == 1)
         def _():
-            for begin in (0, 2):
+            for begin in (0, 1):
                 for d in (2, 3, 1):
-                    early(1, begin, 2, d).start()
+                    early(1, begin, 1, d).start()
 
         return 0
 
@@ -358,14 +359,14 @@
             src_ref=blocks.at[pl.ds(20 * to_c + 8 * to_h + begin, count), :, rows],
             dst_ref=got1.at[pl.ds(begin, count), pz, :, rows],
             send_sem=s1.at[0],
-            recv_sem=r0.at[part + begin // 2],
+            recv_sem=r0.at[part + begin],
             device_id=at(i, to_h, to_c),
             device_id_type=MESH,
         )
 
     def early_come(part, begin, count):
         await_bytes(
-            got1.at[pl.ds(begin, count), pl.ds(0, 3), :, pl.ds(16 * part, 16)], r0.at[part + begin // 2]
+            got1.at[pl.ds(begin, count), pl.ds(0, 3), :, pl.ds(16 * part, 16)], r0.at[part + begin]
         )
 
     greet()
@@ -388,7 +389,7 @@
             first(pair, d).start()
         return 0
 
-    lax.fori_loop(2, PAIRS, send_first, 0)
+    lax.fori_loop(1, PAIRS, send_first, 0)
 
     def second(pair, d):
         to_i, to_c = (i + d // 2) % 4, (c + d % 2) % 2
@@ -400,6 +401,20 @@
             device_id=at(to_i, h, to_c),
             device_id_type=MESH,
         )
+
+    def single(k, d):
+        to_i, to_c = (i + d // 2) % 4, (c + d % 2) % 2
+        return pltpu.make_async_remote_copy(
+            src_ref=rows2.at[k, 2 * to_i + to_c],
+            dst_ref=got2.at[k, 4 * c + i],
+            send_sem=s2.at[0],
+            recv_sem=r3.at[k % 2 + 2 * (k // 8)],
+            device_id=at(to_i, h, to_c),
+            device_id_type=MESH,
+        )
+
+    def single_come(k):
+        await_bytes(got2.at[k, pl.ds(0, 7)], r3.at[k % 2 + 2 * (k // 8)])
 
     lane = lax.broadcasted_iota(jnp.int32, (128, 128), 1)
     lane_low = lane < 64
@@ -535,42 +550,65 @@
     def rounds(step, _):
         @pl.when(step == 0)
         def _():
-            early_come(0, 0, 4)
-            early_come(1, 0, 2)
-
-        @pl.when(step == 1)
-        def _():
-            early_come(1, 2, 2)
-
-        @pl.when(jnp.logical_and(step > 1, step < PAIRS))
-        def _():
-            await_bytes(got1.at[pl.ds(2 * step, 2), pl.ds(0, 3)], r1.at[step])
-
-        @pl.when(step < PAIRS)
+            early_come(0, 0, 2)
+
+        @pl.when(step > 0)
+        def _():
+            @pl.when(step < PAIRS)
+            def _():
+                await_bytes(got1.at[pl.ds(2 * step, 2), pl.ds(0, 3)], r1.at[step])
+
+        @pl.when(jnp.logical_or(step == 0, step == PAIRS - 1))
+        def _():
+            def one(k, _):
+                for begin in (0, 1):
+
+                    @pl.when(k == begin)
+                    def _():
+                        early_come(1, begin, 1)
+
+                b_contraction(k)
+                for d in (4, 5, 2, 6, 3, 7, 1):
+                    single(k, d).start()
+                return 0
+
+            lax.fori_loop(2 * step, 2 * step + 2, one, 0)
+
+        @pl.when(jnp.logical_and(step > 0, step < PAIRS - 1))
         def _():
             for sub in range(2):
                 b_contraction(2 * step + sub)
             for d in (4, 5, 2, 6, 3, 7, 1):
                 second(step, d).start()
 
-        @pl.when(step > 0)
+        @pl.when(step == 1)
+        def _():
+            for k in range(2):
+                single_come(k)
+                a_contraction(k)
+                transport(k, True)
+
+        @pl.when(jnp.logical_and(step > 1, step < PAIRS))
         def _():
             await_bytes(got2.at[pl.ds(2 * step - 2, 2), pl.ds(0, 7)], r2.at[step - 1])
             for sub in range(2):
                 a_contraction(2 * step - 2 + sub)
 
-        @pl.when(step == 1)
-        def _():
-            for k in range(2):
-                transport(k, True)
-
-        @pl.when(step > 1)
-        def _():
             def one(sub, _):
                 transport(2 * step - 2 + sub, False)
                 return 0
 
             lax.fori_loop(0, 2, one, 0)
+
+        @pl.when(step == PAIRS)
+        def _():
+            def one(k, _):
+                single_come(k)
+                a_contraction(k)
+                transport(k, False)
+                return 0
+
+            lax.fori_loop(2 * PAIRS - 2, 2 * PAIRS, one, 0)
 
         return 0
 
@@ -718,6 +756,7 @@
             dma((1,)),
             dma((PAIRS,)),
             dma((4,)),
+            dma((4,)),
             dma((3,)),
             dma((4, 2)),
             dma((5,)),

time: 87.3 us -> 81.9 us (0.938)
  Pallas kernels: 85.2 us -> 79.9 us
    pallas_call x1, Pallas kernels: 85.2 us -> 79.9 us  [local(): pl.pallas_call(kernel, out_shape=jax.ShapeDtypeStruct((512, 256), F32), i...]
where the time goes in v10:
time: 81.9 us; the launch traced here: 81.8 us
  Pallas kernels  79.9 us (98%)
  local copies, waits for them, and re-layouts  1.87 us (2%)
    pallas_call x1, Pallas kernels, local(): pl.pallas_call(kernel, out_shape=jax.ShapeDtypeStruct((512, 256), F32), i...  79.9 us
    unnamed x1, local copies, waits for them, and re-layouts  1.87 us

profile of v10, /device:TPU:1, one launch (start us, length us, event | category | flops | bytes accessed | tf_op | source)
XLA Modules:
  0.0 81.8 jit_solution(15629447711669341183)
XLA Ops:
  0.0 79.9 %shard_map.91 = f32[512,256]{1,0:T(8,128)} custom-call(s32[2,3]{1,0:T(2,128)} %point.1, f32[256]{0:T(256)} %prof.1, f32[64,64,256]{2,1,0:T(8,128)} %xi_far.1, bf16[3,64,64,256]{3,2,1,0:T(8,128)(2,1)} %basis_far.1, f32[4096,256]{1,0:T(8,128)} %bitcast.2, s32[256,256]{1,0:T(8,128)} %mask_far.1, bf16[8,256,128]{2,1,0:T(8,128)(2,1)} %constant.6.clone.tz_far, ...), custom_call_target="tpu_custom_call" | custom-call | tf_op jit(solution)/shard_map/pallas_call | solution.py:722
  79.9 1.9 %copy.11 = f32[32,16,256]{2,1,0:T(8,128)} copy(f32[32,16,256]{2,1,0:T(8,128)} %bitcast.3) | data formatting | bytes 1048576

commit v11 on v10

--- a/solution.py
+++ b/solution.py
@@ -41,13 +41,13 @@
                 if z >= 0:
                     tz[g, 20 * par + w] = full[z]
     tz = tz.transpose(0, 2, 1)
-    cy = np.zeros((8, 5, 8, G))
+    cy = np.zeros((8, 40, G))
     for u in range(8):
         for t in range(5):
             for q in range(8):
                 y = 32 * u - 8 + 5 * q + t
-                if y >= 0:
-                    cy[u, t, q] = full[y]
+                if y >= 0 and (t == 4 or q > 0):
+                    cy[u, q if t == 4 else 7 + 7 * t + q] = full[y]
     cx = 0.5 * np.concatenate([full[0::2], full[1::2]], axis=0).T
     return split_table(tz), split_table(cy.reshape(320, G)), split_table(cx)
 
@@ -439,7 +439,7 @@
         rest = lax.dot_general(cy[0:320], low, NT, preferred_element_type=F32)
         total = both[0:320] + both[320:640] + rest
         for slab in range(8):
-            rows2[k, slab] = total[40 * slab : 40 * slab + 40]
+            rows2[k, slab] = total[40 * slab : 40 * slab + 36]
         got2[k, 4 * c + i] = rows2[k, u]
 
     def a_contraction(k):
@@ -448,8 +448,16 @@
             for pair in range(2):
                 cols = [[], []]
                 for group in range(2):
-                    one = got2[k, 4 * core + 2 * group, :, 128 * pair : 128 * pair + 128]
-                    two = got2[k, 4 * core + 2 * group + 1, :, 128 * pair : 128 * pair + 128]
+                    one, two = (
+                        jnp.concatenate(
+                            [
+                                got2[k, 4 * core + 2 * group + m, first_row : first_row + 8, 128 * pair : 128 * pair + 128]
+                                for first_row in (7, 14, 21, 28, 0)
+                            ],
+                            axis=0,
+                        )
+                        for m in range(2)
+                    )
                     cols[0].append(jnp.where(lane40, one, pltpu.roll(two, 64, 1)))
                     cols[1].append(jnp.where(lane40, pltpu.roll(one, 64, 1), two))
                 rows += [jnp.concatenate(col, axis=1) for col in cols]
@@ -547,6 +555,59 @@
                 cz.at[:, pl.ds(0, 20), pl.ds(8, 8)], conc0.at[:, :, pl.ds(0, 8)], rc.at[2]
             ).wait()
 
+    granule = lax.broadcasted_iota(jnp.int32, (8, 128), 1) // 16
+    zr = 16 * (4 * yy + 2 * xt + h)
+
+    def home(zp, dp, half):
+        to = (pts + dp) % 8
+        return pltpu.make_async_remote_copy(
+            src_ref=parcel.at[zp, to, half],
+            dst_ref=landed.at[:, pl.ds(pl.multiple_of(zr + 8 * zp, 8), 8)],
+            send_sem=so.at[3 * zp + (0 if dp else 1 + half)],
+            recv_sem=ro.at[zp],
+            device_id={"pts": to, "py": i, "pz": 2 * c + half},
+            device_id_type=MESH,
+        )
+
+    def home_own(zp, half):
+        return pltpu.make_async_copy(
+            parcel.at[zp, pts, half], landed.at[:, pl.ds(pl.multiple_of(zr + 8 * zp, 8), 8)], ro.at[zp]
+        )
+
+    def go_home(zp):
+        def regroup(which, _):
+            half, yg = which // 4, which % 4
+            arrays = []
+            for y in range(4):
+                for v in range(2):
+                    row = pl.multiple_of(16 * (8 + 16 * half + 4 * yg + y) + 8 * zp, 8)
+                    arrays.append(sums[v, pl.ds(row, 8), :])
+            for bit in (4, 2, 1):
+                clear = (granule // bit) % 2 == 0
+                for m in range(8):
+                    if m // bit % 2 == 0:
+                        one, two = arrays[m], arrays[m + bit]
+                        arrays[m] = jnp.where(clear, one, pltpu.roll(two, 16 * bit, 1))
+                        arrays[m + bit] = jnp.where(clear, pltpu.roll(one, 128 - 16 * bit, 1), two)
+            for p in range(8):
+                parcel[zp, p, half, yg] = arrays[p]
+            return 0
+
+        for half in range(2):
+            lax.fori_loop(4 * half, 4 * half + 4, regroup, 0)
+            here = jnp.logical_and(c == h, c == half)
+
+            @pl.when(here)
+            def _():
+                home_own(zp, half).start()
+
+            @pl.when(jnp.logical_not(here))
+            def _():
+                home(zp, 0, half).start()
+
+            for dp in range(1, 8):
+                home(zp, dp, half).start()
+
     def rounds(step, _):
         @pl.when(step == 0)
         def _():
@@ -599,6 +660,10 @@
                 return 0
 
             lax.fori_loop(0, 2, one, 0)
+
+        @pl.when(step == 3)
+        def _():
+            go_home(0)
 
         @pl.when(step == PAIRS)
         def _():
@@ -621,58 +686,9 @@
             nodes[n, r] = jnp.broadcast_to(listed[n // 2, row : row + 1, :], (8, 128))
     lax.fori_loop(0, PAIRS + 1, rounds, 0)
 
-    granule = lax.broadcasted_iota(jnp.int32, (16, 128), 1) // 16
-
-    def regroup(which, _):
-        half, yg = which // 4, which % 4
-        arrays = []
-        for yy in range(4):
-            for v in range(2):
-                row = pl.multiple_of(16 * (8 + 16 * half + 4 * yg + yy), 16)
-                arrays.append(sums[v, pl.ds(row, 16), :])
-        for bit in (4, 2, 1):
-            clear = (granule // bit) % 2 == 0
-            for m in range(8):
-                if m // bit % 2 == 0:
-                    one, two = arrays[m], arrays[m + bit]
-                    arrays[m] = jnp.where(clear, one, pltpu.roll(two, 16 * bit, 1))
-                    arrays[m + bit] = jnp.where(clear, pltpu.roll(one, 128 - 16 * bit, 1), two)
-        for p in range(8):
-            parcel[p, half, yg] = arrays[p]
-        return 0
-
-    zr = pl.multiple_of(16 * (4 * yy + 2 * xt + h), 16)
-
-    def home(dp, half):
-        to = (pts + dp) % 8
-        return pltpu.make_async_remote_copy(
-            src_ref=parcel.at[to, half],
-            dst_ref=landed.at[:, pl.ds(zr, 16)],
-            send_sem=so.at[0 if dp else 1 + half],
-            recv_sem=ro.at[0],
-            device_id={"pts": to, "py": i, "pz": 2 * c + half},
-            device_id_type=MESH,
-        )
-
-    def home_own(half):
-        return pltpu.make_async_copy(parcel.at[pts, half], landed.at[:, pl.ds(zr, 16)], ro.at[0])
-
-    for half in range(2):
-        lax.fori_loop(4 * half, 4 * half + 4, regroup, 0)
-        here = jnp.logical_and(c == h, c == half)
-
-        @pl.when(here)
-        def _():
-            home_own(half).start()
-
-        @pl.when(jnp.logical_not(here))
-        def _():
-            home(0, half).start()
-
-        for dp in range(1, 8):
-            home(dp, half).start()
-
-    await_bytes(landed, ro.at[0])
+    go_home(1)
+    for zp in range(2):
+        await_bytes(landed.at[:, pl.ds(0, 128)], ro.at[zp])
 
     for yg in range(4):
         for zh in range(2):
@@ -687,12 +703,14 @@
     await_bytes(share.at[pl.ds(0, 3 * 128 * NROUND)], s1.at[0])
     await_bytes(rows2.at[:, pl.ds(0, 7)], s2.at[0])
     await_bytes(listed.at[pl.ds(0, 7)], sn.at[0])
-    await_bytes(parcel.at[pl.ds(0, 7)], so.at[0])
+    for zp in range(2):
+        await_bytes(parcel.at[zp, pl.ds(0, 7)], so.at[3 * zp])
     for half in range(2):
 
         @pl.when(jnp.logical_not(jnp.logical_and(c == h, c == half)))
         def _():
-            home(0, half).wait_send()
+            for zp in range(2):
+                home(zp, 0, half).wait_send()
 
     for to_h in range(2):
 
@@ -729,8 +747,8 @@
             pltpu.VMEM((3, 64, 64, 256), BF16),
             pltpu.VMEM((40 * 128, 128), F32),
             pltpu.VMEM((NROUND, 4, 4, 32, 128), F32),
-            pltpu.VMEM((NROUND, 8, 40, 256), F32),
-            pltpu.VMEM((NROUND, 8, 40, 256), F32),
+            pltpu.VMEM((NROUND, 8, 36, 256), F32),
+            pltpu.VMEM((NROUND, 8, 36, 256), F32),
             pltpu.VMEM((2, 20, 40, 128), F32),
             pltpu.VMEM((2, 2, 4, 40, 256), F32),
             pltpu.VMEM((POINTS, STEPS, 5, 2, 8, 128), F32),
@@ -740,7 +758,7 @@
             pltpu.VMEM((8, 8, 128), F32),
             pltpu.VMEM((POINTS, 4, 8, 128), F32),
             pltpu.VMEM((2, 640, 128), F32),
-            pltpu.VMEM((8, 2, 4, 16, 128), F32),
+            pltpu.VMEM((2, 8, 2, 4, 8, 128), F32),
             pltpu.VMEM((4, 256, 128), F32),
             pltpu.VMEM((2, 512, 128), F32),
             pltpu.VMEM((256, 128), BF16),
@@ -761,8 +779,8 @@
             dma((4, 2)),
             dma((5,)),
             dma((2,)),
-            dma((3,)),
-            dma((1,)),
+            dma((6,)),
+            dma((2,)),
         ],
         compiler_params=pltpu.CompilerParams(
             collective_id=0, has_side_effects=True, vmem_limit_bytes=60 * 2**20

time: 81.9 us -> 79.7 us (0.973)
  Pallas kernels: 79.9 us -> 77.7 us
    pallas_call x1, Pallas kernels: 79.9 us -> 77.7 us  [local(): pl.pallas_call(kernel, out_shape=jax.ShapeDtypeStruct((512, 256), F32), i...]
where the time goes in v11:
time: 79.7 us; the launch traced here: 79.6 us
  Pallas kernels  77.7 us (97%)
  local copies, waits for them, and re-layouts  1.87 us (2%)
    pallas_call x1, Pallas kernels, local(): pl.pallas_call(kernel, out_shape=jax.ShapeDtypeStruct((512, 256), F32), i...  77.7 us
    unnamed x1, local copies, waits for them, and re-layouts  1.87 us

profile of v11, /device:TPU:1, one launch (start us, length us, event | category | flops | bytes accessed | tf_op | source)
XLA Modules:
  0.0 79.6 jit_solution(6547242992306743745)
XLA Ops:
  0.0 77.7 %shard_map.91 = f32[512,256]{1,0:T(8,128)} custom-call(s32[2,3]{1,0:T(2,128)} %point.1, f32[256]{0:T(256)} %prof.1, f32[64,64,256]{2,1,0:T(8,128)} %xi_far.1, bf16[3,64,64,256]{3,2,1,0:T(8,128)(2,1)} %basis_far.1, f32[4096,256]{1,0:T(8,128)} %bitcast.2, s32[256,256]{1,0:T(8,128)} %mask_far.1, bf16[8,256,128]{2,1,0:T(8,128)(2,1)} %constant.6.clone.tz_far, ...), custom_call_target="tpu_custom_call" | custom-call | tf_op jit(solution)/shard_map/pallas_call | solution.py:740
  77.7 1.9 %copy.11 = f32[32,16,256]{2,1,0:T(8,128)} copy(f32[32,16,256]{2,1,0:T(8,128)} %bitcast.3) | data formatting | bytes 1048576

commit v12 on v11

--- a/solution.py
+++ b/solution.py
@@ -98,7 +98,6 @@
     s1,
     r1,
     s2,
-    r2,
     r3,
     sc,
     rc,
@@ -391,30 +390,19 @@
 
     lax.fori_loop(1, PAIRS, send_first, 0)
 
-    def second(pair, d):
-        to_i, to_c = (i + d // 2) % 4, (c + d % 2) % 2
-        return pltpu.make_async_remote_copy(
-            src_ref=rows2.at[pl.ds(2 * pair, 2), 2 * to_i + to_c],
-            dst_ref=got2.at[pl.ds(2 * pair, 2), 4 * c + i],
-            send_sem=s2.at[0],
-            recv_sem=r2.at[pair],
-            device_id=at(to_i, h, to_c),
-            device_id_type=MESH,
-        )
-
     def single(k, d):
         to_i, to_c = (i + d // 2) % 4, (c + d % 2) % 2
         return pltpu.make_async_remote_copy(
             src_ref=rows2.at[k, 2 * to_i + to_c],
             dst_ref=got2.at[k, 4 * c + i],
             send_sem=s2.at[0],
-            recv_sem=r3.at[k % 2 + 2 * (k // 8)],
+            recv_sem=r3.at[k],
             device_id=at(to_i, h, to_c),
             device_id_type=MESH,
         )
 
     def single_come(k):
-        await_bytes(got2.at[k, pl.ds(0, 7)], r3.at[k % 2 + 2 * (k // 8)])
+        await_bytes(got2.at[k, pl.ds(0, 7)], r3.at[k])
 
     lane = lax.broadcasted_iota(jnp.int32, (128, 128), 1)
     lane_low = lane < 64
@@ -608,72 +596,47 @@
             for dp in range(1, 8):
                 home(zp, dp, half).start()
 
+    lag = 3
+
     def rounds(step, _):
         @pl.when(step == 0)
         def _():
             early_come(0, 0, 2)
-
-        @pl.when(step > 0)
-        def _():
-            @pl.when(step < PAIRS)
+            early_come(1, 0, 1)
+
+        @pl.when(step == 1)
+        def _():
+            early_come(1, 1, 1)
+
+        for pair in range(1, PAIRS):
+
+            @pl.when(step == 2 * pair)
             def _():
-                await_bytes(got1.at[pl.ds(2 * step, 2), pl.ds(0, 3)], r1.at[step])
-
-        @pl.when(jnp.logical_or(step == 0, step == PAIRS - 1))
-        def _():
-            def one(k, _):
-                for begin in (0, 1):
-
-                    @pl.when(k == begin)
-                    def _():
-                        early_come(1, begin, 1)
-
-                b_contraction(k)
-                for d in (4, 5, 2, 6, 3, 7, 1):
-                    single(k, d).start()
-                return 0
-
-            lax.fori_loop(2 * step, 2 * step + 2, one, 0)
-
-        @pl.when(jnp.logical_and(step > 0, step < PAIRS - 1))
-        def _():
-            for sub in range(2):
-                b_contraction(2 * step + sub)
+                await_bytes(got1.at[pl.ds(2 * pair, 2), pl.ds(0, 3)], r1.at[pair])
+
+        @pl.when(step < NROUND)
+        def _():
+            b_contraction(step)
             for d in (4, 5, 2, 6, 3, 7, 1):
-                second(step, d).start()
-
-        @pl.when(step == 1)
-        def _():
-            for k in range(2):
+                single(step, d).start()
+
+        for k in range(2):
+
+            @pl.when(step == lag + k)
+            def _():
                 single_come(k)
                 a_contraction(k)
                 transport(k, True)
 
-        @pl.when(jnp.logical_and(step > 1, step < PAIRS))
-        def _():
-            await_bytes(got2.at[pl.ds(2 * step - 2, 2), pl.ds(0, 7)], r2.at[step - 1])
-            for sub in range(2):
-                a_contraction(2 * step - 2 + sub)
-
-            def one(sub, _):
-                transport(2 * step - 2 + sub, False)
-                return 0
-
-            lax.fori_loop(0, 2, one, 0)
-
-        @pl.when(step == 3)
+        @pl.when(step >= lag + 2)
+        def _():
+            single_come(step - lag)
+            a_contraction(step - lag)
+            transport(step - lag, False)
+
+        @pl.when(step == lag + 5)
         def _():
             go_home(0)
-
-        @pl.when(step == PAIRS)
-        def _():
-            def one(k, _):
-                single_come(k)
-                a_contraction(k)
-                transport(k, False)
-                return 0
-
-            lax.fori_loop(2 * PAIRS - 2, 2 * PAIRS, one, 0)
 
         return 0
 
@@ -684,7 +647,7 @@
         for r in range(4):
             row = 4 * (n % 2) + r
             nodes[n, r] = jnp.broadcast_to(listed[n // 2, row : row + 1, :], (8, 128))
-    lax.fori_loop(0, PAIRS + 1, rounds, 0)
+    lax.fori_loop(0, NROUND + lag, rounds, 0)
 
     go_home(1)
     for zp in range(2):
@@ -772,8 +735,7 @@
             dma((1,)),
             dma((PAIRS,)),
             dma((1,)),
-            dma((PAIRS,)),
-            dma((4,)),
+            dma((NROUND,)),
             dma((4,)),
             dma((3,)),
             dma((4, 2)),

time: 79.7 us -> 77.7 us (0.975)
  Pallas kernels: 77.7 us -> 75.6 us
    pallas_call x1, Pallas kernels: 77.7 us -> 75.6 us  [local(): pl.pallas_call(kernel, out_shape=jax.ShapeDtypeStruct((512, 256), F32), i...]
where the time goes in v12:
time: 77.7 us; the launch traced here: 77.5 us
  Pallas kernels  75.6 us (97%)
  local copies, waits for them, and re-layouts  1.87 us (2%)
    pallas_call x1, Pallas kernels, local(): pl.pallas_call(kernel, out_shape=jax.ShapeDtypeStruct((512, 256), F32), i...  75.6 us
    unnamed x1, local copies, waits for them, and re-layouts  1.87 us

profile of v12, /device:TPU:1, one launch (start us, length us, event | category | flops | bytes accessed | tf_op | source)
XLA Modules:
  0.0 77.5 jit_solution(3777455239386196094)
XLA Ops:
  0.0 75.6 %shard_map.91 = f32[512,256]{1,0:T(8,128)} custom-call(s32[2,3]{1,0:T(2,128)} %point.1, f32[256]{0:T(256)} %prof.1, f32[64,64,256]{2,1,0:T(8,128)} %xi_far.1, bf16[3,64,64,256]{3,2,1,0:T(8,128)(2,1)} %basis_far.1, f32[4096,256]{1,0:T(8,128)} %bitcast.2, s32[256,256]{1,0:T(8,128)} %mask_far.1, bf16[8,256,128]{2,1,0:T(8,128)(2,1)} %constant.6.clone.tz_far, ...), custom_call_target="tpu_custom_call" | custom-call | tf_op jit(solution)/shard_map/pallas_call | solution.py:703
  75.6 1.9 %copy.11 = f32[32,16,256]{2,1,0:T(8,128)} copy(f32[32,16,256]{2,1,0:T(8,128)} %bitcast.3) | data formatting | bytes 1048576

commit v13 on v12

--- a/solution.py
+++ b/solution.py
@@ -346,6 +346,9 @@
             for begin in (0, 1):
                 for d in (2, 3, 1):
                     early(1, begin, 1, d).start()
+            for k in (2, 3):
+                for d in (2, 3, 1):
+                    lone(k, d).start()
 
         return 0
 
@@ -363,6 +366,17 @@
             device_id_type=MESH,
         )
 
+    def lone(k, d):
+        to_h, to_c = (h + d // 2) % 2, (c + d % 2) % 2
+        return pltpu.make_async_remote_copy(
+            src_ref=blocks.at[20 * to_c + 8 * to_h + k],
+            dst_ref=got1.at[k, pz],
+            send_sem=s1.at[0],
+            recv_sem=r0.at[1 + k],
+            device_id=at(i, to_h, to_c),
+            device_id_type=MESH,
+        )
+
     def early_come(part, begin, count):
         await_bytes(
             got1.at[pl.ds(begin, count), pl.ds(0, 3), :, pl.ds(16 * part, 16)], r0.at[part + begin]
@@ -388,7 +402,7 @@
             first(pair, d).start()
         return 0
 
-    lax.fori_loop(1, PAIRS, send_first, 0)
+    lax.fori_loop(2, PAIRS, send_first, 0)
 
     def single(k, d):
         to_i, to_c = (i + d // 2) % 4, (c + d % 2) % 2
@@ -608,7 +622,13 @@
         def _():
             early_come(1, 1, 1)
 
-        for pair in range(1, PAIRS):
+        for k in (2, 3):
+
+            @pl.when(step == k)
+            def _():
+                await_bytes(got1.at[k, pl.ds(0, 3)], r0.at[1 + k])
+
+        for pair in range(2, PAIRS):
 
             @pl.when(step == 2 * pair)
             def _():
@@ -731,7 +751,7 @@
             pltpu.VMEM((2, 256, 128), jnp.int32),
             pltpu.VMEM((2, 264, 128), F32),
             pltpu.VMEM((2, 40, 128), F32),
-            dma((3,)),
+            dma((5,)),
             dma((1,)),
             dma((PAIRS,)),
             dma((1,)),

time: 77.7 us -> 77.7 us (level)
  no operation moved by 1% of the time
where the time goes in v13:
time: 77.7 us; the launch traced here: 77.5 us
  Pallas kernels  75.6 us (97%)
  local copies, waits for them, and re-layouts  1.87 us (2%)
    pallas_call x1, Pallas kernels, local(): pl.pallas_call(kernel, out_shape=jax.ShapeDtypeStruct((512, 256), F32), i...  75.6 us
    unnamed x1, local copies, waits for them, and re-layouts  1.87 us

profile of v13, /device:TPU:1, one launch (start us, length us, event | category | flops | bytes accessed | tf_op | source)
XLA Modules:
  0.0 77.5 jit_solution(14165518808732737943)
XLA Ops:
  0.0 75.6 %shard_map.91 = f32[512,256]{1,0:T(8,128)} custom-call(s32[2,3]{1,0:T(2,128)} %point.1, f32[256]{0:T(256)} %prof.1, f32[64,64,256]{2,1,0:T(8,128)} %xi_far.1, bf16[3,64,64,256]{3,2,1,0:T(8,128)(2,1)} %basis_far.1, f32[4096,256]{1,0:T(8,128)} %bitcast.2, s32[256,256]{1,0:T(8,128)} %mask_far.1, bf16[8,256,128]{2,1,0:T(8,128)(2,1)} %constant.6.clone.tz_far, ...), custom_call_target="tpu_custom_call" | custom-call | tf_op jit(solution)/shard_map/pallas_call | solution.py:723
  75.6 1.9 %copy.11 = f32[32,16,256]{2,1,0:T(8,128)} copy(f32[32,16,256]{2,1,0:T(8,128)} %bitcast.3) | data formatting | bytes 1048576
